TPU v7x, 256 devices: a whole 4x4x8 slice. The times are simulated.
256 devices in a mesh: slab: 32 (over z, y), lat: 8 (over x, core).
Axes of the slice: x: 4, y: 4, z: 8, core: 2. Of those that a mesh axis runs over, the one named last changes fastest.
Arguments:
- density: float32 [128, 512, 1024], P('slab', 'lat'), may hold values from 0.05 to 2
- bins: int32 [128, 512, 1024], P('slab', 'lat'), may hold values from 0 to 255
- transfer: bfloat16 [4, 256], replicated, may hold values from 0.099609375 to 1.5
- depth_order: int32 [512, 1024], P('lat'), may hold values 0 or 1
Outputs:
- frame: float32 [4, 512, 1024], P(None, ('lat', 'slab'))
All inputs are finite; a program needn't handle non-finite values. No bound on the sum of `depth_order` on one device may be relied on, other than what follows from the above.
Results may differ from a plain program's by a relative error of at most 0.0003.
Values sent between devices are 32-bit elements; how exact they have to be, the bound alone decides.
No kernel may reach another device: no remote copies, remote signals or barrier semaphores. Data moves between devices by JAX's collectives and lax.ppermute only.
A program may use at most 64 MiB of HBM per device.

v0:
```python
import math

import jax
import jax.numpy as jnp
from jax import lax
from jax.sharding import PartitionSpec as P

LIGHT_X = 0.48
LIGHT_Y = 0.6
LIGHT_Z = 0.64


def with_halo(block, sides, width):
    for axis, dim in sides:
        count = lax.axis_size(axis)
        forward = [(i, i + 1) for i in range(count - 1)]
        backward = [(target, source) for source, target in forward]
        low = lax.ppermute(
            lax.slice_in_dim(block, block.shape[dim] - width, None, axis=dim), axis, forward
        )
        high = lax.ppermute(lax.slice_in_dim(block, 0, width, axis=dim), axis, backward)
        block = jnp.concatenate([low, block, high], axis=dim)
    return block


def from_partner(block, axis, stride):
    count = lax.axis_size(axis)
    route = []
    for low in range(count):
        high = low | 1 << stride
        if high != low and high < count:
            route += [(low, high), (high, low)]
    return lax.ppermute(block, axis, route)


def shading_of(padded):
    center = padded[1:-1, 1:-1, 1:-1]
    slope_z = (padded[2:, 1:-1, 1:-1] - padded[:-2, 1:-1, 1:-1]) * 0.5
    slope_y = (padded[1:-1, 2:, 1:-1] - padded[1:-1, :-2, 1:-1]) * 0.5
    slope_x = (padded[1:-1, 1:-1, 2:] - padded[1:-1, 1:-1, :-2]) * 0.5
    facing = LIGHT_X * slope_x + LIGHT_Y * slope_y + LIGHT_Z * slope_z
    shading = 1.0 + facing / jnp.sqrt(
        slope_x * slope_x + slope_y * slope_y + slope_z * slope_z + 0.25
    )
    return (center, shading)


def march(optical, radiance):
    running = jnp.cumsum(optical, axis=0)
    overall = running[-1]
    ahead = jnp.exp(optical - running)
    behind = jnp.exp(running - overall)
    front_rgb = jnp.sum(radiance * ahead[None], axis=1)
    back_rgb = jnp.sum(radiance * behind[None], axis=1)
    return (front_rgb, back_rgb, overall)


def shards(density, bins, transfer, depth_order):
    depth_cells, row_cells, line_cells = density.shape
    slab_count = lax.axis_size("slab")
    position = lax.axis_index("slab")
    spacing = 1.5 / (depth_cells * slab_count)
    extended = with_halo(density, (("slab", 0), ("lat", 1)), 1)
    padded = jnp.pad(extended, ((0, 0), (0, 0), (1, 1)))
    center, shading = shading_of(padded)
    cell_count = depth_cells * row_cells * line_cells
    block_cells = math.gcd(cell_count, 65536)
    label_rows = bins.reshape(cell_count // block_cells, block_cells)
    levels = jnp.arange(transfer.shape[1], dtype=jnp.int32)

    def lookup(labels):
        one_hot = (labels[:, None] == levels[None, :]).astype(jnp.bfloat16)
        return lax.dot_general(
            transfer, one_hot, (((1,), (1,)), ((), ())), preferred_element_type=jnp.float32
        )

    looked_up = lax.map(lookup, label_rows)
    brick_shape = (depth_cells, row_cells, line_cells)
    extinction = looked_up[:, 3, :].reshape(brick_shape)
    emission = jnp.stack([looked_up[:, k, :].reshape(brick_shape) for k in range(3)], axis=0)
    optical = extinction * center * spacing
    radiance = emission * (shading * (1.0 - jnp.exp(-optical)))[None]
    front_rgb, back_rgb, overall = march(optical, radiance)
    reverse_mask = depth_order == 1
    own_rgb = jnp.where(reverse_mask[None], back_rgb, front_rgb)
    own_light = jnp.exp(-overall)
    row_share = row_cells // slab_count
    partial_value = jnp.concatenate([own_rgb, own_light[None]], axis=0)
    partial_value = partial_value.reshape(4, slab_count, row_share, line_cells)
    masks = reverse_mask.reshape(slab_count, row_share, line_cells)
    rounds = slab_count.bit_length() - 1
    groups = slab_count
    for b in range(rounds):
        own_bit = position >> b & 1
        paired = partial_value.reshape(4, groups // 2, 2, row_share, line_cells)
        first_of = paired[:, :, 0]
        second_of = paired[:, :, 1]
        retained = jnp.where(own_bit == 0, first_of, second_of)
        outgoing = jnp.where(own_bit == 0, second_of, first_of)
        incoming = from_partner(outgoing, "slab", b)
        lower_half = jnp.where(own_bit == 0, retained, incoming)
        upper_half = jnp.where(own_bit == 0, incoming, retained)
        paired_mask = masks.reshape(groups // 2, 2, row_share, line_cells)
        masks = jnp.where(own_bit == 0, paired_mask[:, 0], paired_mask[:, 1])
        in_front = jnp.where(masks[None], upper_half, lower_half)
        behind_it = jnp.where(masks[None], lower_half, upper_half)
        partial_value = jnp.concatenate(
            [in_front[0:3] + in_front[3:4] * behind_it[0:3], in_front[3:4] * behind_it[3:4]], axis=0
        )
        groups = groups // 2
    partial_value = partial_value.reshape(4, row_share, line_cells)
    colors = partial_value[0:3]
    opacity = 1.0 - partial_value[3]
    return jnp.concatenate([colors, opacity[None]], axis=0)


def solution(mesh):
    return jax.shard_map(
        shards,
        mesh=mesh,
        in_specs=(P("slab", "lat", None), P("slab", "lat", None), P(), P("lat", None)),
        out_specs=P(None, ("lat", "slab"), None),
        check_vma=False,
    )
```

profile of v0, /device:TPU:2, one launch (start us, length us, event | category | flops | bytes accessed | tf_op | source)
XLA Modules:
  0.0 171.3 jit_solution(6487238040825361100)
XLA Ops:
  0.0 1.9 %fusion.33 = (f32[1,64,1024]{2,1,0:T(8,128)}, f32[1,64,1024]{2,1,0:T(8,128)}) fusion(f32[4,64,1024]{2,1,0:T(8,128)} %param.6), kind=kLoop, calls=%fused_computation.125 | loop fusion | bytes 1048576 | tf_op jit(solution)/shard_map/slice | solution.py:21
  1.9 3.5 %collective-permute-start = (f32[1,64,1024]{2,1,0:T(8,128)}, f32[1,64,1024]{2,1,0:T(8,128)S(1)}, u32[]{:S(2)}, u32[]{:S(2)}) collective-permute-start(f32[1,64,1024]{2,1,0:T(8,128)} %get-tuple-element.69), channel_id=1, source_target_pairs={{0,8},{8,16},{16,24},{24,32},{32,40},{40,48},{48,56},{56,64},{64,7... | collective-permute-start | bytes 786440 | tf_op jit(solution)/shard_map/ppermute | solution.py:18
  5.4 1.3 collective-permute-start.1
  6.7 1.9 %copy.91 = s32[1,4,64,1024]{3,1,2,0:T(4,128)S(1)} copy(s32[1,4,64,1024]{3,2,1,0:T(8,128)} %bitcast.215) | data formatting | bytes 2097152
  8.6 67.4 %while.11 = (s32[]{:T(128)}, f32[4,4,65536]{2,1,0:T(4,128)}, s32[4,65536]{1,0:T(4,128)S(1)}, bf16[4,256]{1,0:T(4,128)(2,1)S(1)}, s32[]{:T(128)}) while((s32[]{:T(128)}, f32[4,4,65536]{2,1,0:T(4,128)}, s32[4,65536]{1,0:T(4,128)S(1)}, bf16[4,256]{1,0:T(4,128)(2,1)S(1)}, s32[]{:T(128)}) %tuple.49), condition=%wide.region_1.2_spmd.clone, body=%wide.region_0.1_spmd.clone.sunk | while | flops 150994944 | bytes 1837133 | solution.py:77
  8.6 0.2 constant_dynamic-slice_fusion.2
  8.9 16.6 %fusion.41 = f32[4,4,65536]{2,1,0:T(4,128)} fusion(f32[4,4,65536]{2,1,0:T(4,128)} %get-tuple-element.125, s32[]{:T(128)S(6)} %copy.116, bf16[4,256]{1,0:T(4,128)(2,1)S(1)} %get-tuple-element.132, s32[65536]{0:T(1024)S(1)} %bitcast.204), kind=kOutput, calls=%fused_computation.2.clone.2 | convolution fusion | flops 150994944 | bytes 1312772 | tf_op jit(solution)/shard_map/while/body/eval_jaxpr/dot_general | solution.py:73
  25.5 0.2 constant_dynamic-slice_fusion.2
  25.7 16.6 %fusion.41 = f32[4,4,65536]{2,1,0:T(4,128)} fusion(f32[4,4,65536]{2,1,0:T(4,128)} %get-tuple-element.125, s32[]{:T(128)S(6)} %copy.116, bf16[4,256]{1,0:T(4,128)(2,1)S(1)} %get-tuple-element.132, s32[65536]{0:T(1024)S(1)} %bitcast.204), kind=kOutput, calls=%fused_computation.2.clone.2 | convolution fusion | flops 150994944 | bytes 1312772 | tf_op jit(solution)/shard_map/while/body/eval_jaxpr/dot_general | solution.py:73
  42.3 0.2 constant_dynamic-slice_fusion.2
  42.6 16.6 %fusion.41 = f32[4,4,65536]{2,1,0:T(4,128)} fusion(f32[4,4,65536]{2,1,0:T(4,128)} %get-tuple-element.125, s32[]{:T(128)S(6)} %copy.116, bf16[4,256]{1,0:T(4,128)(2,1)S(1)} %get-tuple-element.132, s32[65536]{0:T(1024)S(1)} %bitcast.204), kind=kOutput, calls=%fused_computation.2.clone.2 | convolution fusion | flops 150994944 | bytes 1312772 | tf_op jit(solution)/shard_map/while/body/eval_jaxpr/dot_general | solution.py:73
  59.2 0.2 constant_dynamic-slice_fusion.2
  59.4 16.6 %fusion.41 = f32[4,4,65536]{2,1,0:T(4,128)} fusion(f32[4,4,65536]{2,1,0:T(4,128)} %get-tuple-element.125, s32[]{:T(128)S(6)} %copy.116, bf16[4,256]{1,0:T(4,128)(2,1)S(1)} %get-tuple-element.132, s32[65536]{0:T(1024)S(1)} %bitcast.204), kind=kOutput, calls=%fused_computation.2.clone.2 | convolution fusion | flops 150994944 | bytes 1312772 | tf_op jit(solution)/shard_map/while/body/eval_jaxpr/dot_general | solution.py:73
  76.0 19.5 %slice_reduce_fusion.3 = (f32[4,65536]{1,0:T(4,128)}, f32[4,65536]{1,0:T(4,128)S(1)}, f32[4,65536]{1,0:T(4,128)S(1)}, f32[4,65536]{1,0:T(4,128)S(1)}) fusion(f32[4,4,65536]{2,1,0:T(4,128)} %get-tuple-element.32), kind=kLoop, calls=%fused_computation.34 | loop fusion | bytes 8388608 | tf_op jit(solution)/shard_map/slice | solution.py:80
  95.5 2.5 %copy_bitcast_fusion = (f32[1,4,64,1024]{3,2,1,0:T(8,128)}, f32[1,4,64,1024]{3,2,1,0:T(8,128)}) fusion(f32[1,4,64,1024]{3,1,2,0:T(4,128)S(1)} %bitcast.209, f32[1,4,64,1024]{3,1,2,0:T(4,128)S(1)} %bitcast.210), kind=kLoop, calls=%fused_computation.16 | loop fusion | bytes 4194304 | tf_op jit(solution)/shard_map/stack;reshape;squeeze | solution.py:80
  98.1 0.8 fusion.15
  98.9 0.0 copy-start.8
  98.9 0.8 slice_bitcast_fusion
  99.8 0.1 constant_dynamic-update-slice_fusion.1
  99.8 0.0 collective-permute-done.1
  99.9 1.0 constant_dynamic-update-slice_fusion
  100.8 1.2 copy-done.1
  102.0 0.6 fusion.32
  102.6 1.9 %collective-permute-start.2 = (f32[6,1,1024]{2,1,0:T(1,128)}, f32[6,1,1024]{2,1,0:T(1,128)}, u32[]{:S(2)}, u32[]{:S(2)}) collective-permute-start(f32[6,1,1024]{2,1,0:T(1,128)} %get-tuple-element.64), channel_id=1, source_target_pairs={{0,1},{1,2},{2,3},{3,4},{4,5},{5,6},{6,7},{8,9},{9,10},{10,11},{11... | collective-permute-start | bytes 73736 | tf_op jit(solution)/shard_map/ppermute | solution.py:18
  104.6 3.8 %collective-permute-start.3 = (f32[6,1,1024]{2,1,0:T(1,128)}, f32[6,1,1024]{2,1,0:T(1,128)}, u32[]{:S(2)}, u32[]{:S(2)}) collective-permute-start(f32[6,1,1024]{2,1,0:T(1,128)} %get-tuple-element.63), channel_id=1, source_target_pairs={{1,0},{2,1},{3,2},{4,3},{5,4},{6,5},{7,6},{9,8},{10,9},{11,10},{12... | collective-permute-start | bytes 73736 | tf_op jit(solution)/shard_map/ppermute | solution.py:21
  108.4 0.7 broadcast_compare_fusion
  109.1 1.0 reshape_reshape.4
  110.0 1.1 concatenate.46
  111.1 2.0 %copy.110 = f32[1,4,64,1024]{3,2,1,0:T(8,128)S(1)} copy(f32[1,4,64,1024]{3,1,2,0:T(4,128)} %bitcast.208) | data formatting | bytes 2097152
  113.2 1.6 select_maximum_fusion
  114.8 3.3 %subtract_multiply_fusion = (f32[4,64,1024]{2,1,0:T(8,128)S(1)}, f32[4,64,1024]{2,1,0:T(8,128)S(1)}, f32[4,64,1024]{2,1,0:T(8,128)S(1)}) fusion(f32[4,64,1024]{2,1,0:T(8,128)S(1)} %copy-done, f32[1,64,1024]{2,1,0:T(8,128)S(1)} %copy-done.7, f32[1,64,1024]{2,1,0:T(8,128)} %collective-permute-done.1, f32[6,64,1024]{2,1,0:T(8,128)S(1)} %copy-done.2, ...), kind=kLoop, calls=%fused_computation.30 | loop fusion | flops 7864320 | bytes 10797056 | tf_op jit(solution)/shard_map/mul | solution.py:82
  118.1 0.9 multiply_reduce_fusion
  119.0 0.5 reduce_sum.23
  119.4 0.5 reduce_sum.25
  119.9 0.6 broadcast_select_fusion
  120.5 0.4 fusion.10
  120.9 2.7 %collective-permute-start.4 = (f32[4,16,2,1024]{3,2,1,0:T(2,128)S(1)}, f32[4,16,2,1024]{3,2,1,0:T(2,128)S(1)}, u32[]{:S(2)}, u32[]{:S(2)}) collective-permute-start(f32[4,16,2,1024]{3,2,1,0:T(2,128)S(1)} %fusion.10), channel_id=1, source_target_pairs={{0,8},{8,0},{16,24},{24,16},{32,40},{40,32},{48,56},{56,48},{64,72... | collective-permute-start | bytes 1572872 | tf_op jit(solution)/shard_map/ppermute | solution.py:33
  123.6 0.1 slice_select_fusion
  123.8 0.1 fusion.36
  123.9 11.7 %collective-permute-done.4 = f32[4,16,2,1024]{3,2,1,0:T(2,128)S(1)} collective-permute-done((f32[4,16,2,1024]{3,2,1,0:T(2,128)S(1)}, f32[4,16,2,1024]{3,2,1,0:T(2,128)S(1)}, u32[]{:S(2)}, u32[]{:S(2)}) %collective-permute-start.4) | collective-permute-done | bytes 524320 | tf_op jit(solution)/shard_map/ppermute | solution.py:33
  135.6 0.7 broadcast_select_fusion.4
  136.3 0.1 slice_bitcast_fusion.1
  136.4 0.2 fusion.11
  136.7 0.2 pad_maximum_fusion.5
  136.9 0.1 fusion.13
  137.1 3.4 %collective-permute-start.5 = (f32[4,8,2,1024]{3,2,1,0:T(2,128)S(1)}, f32[4,8,2,1024]{3,2,1,0:T(2,128)S(1)}, u32[]{:S(2)}, u32[]{:S(2)}) collective-permute-start(f32[4,8,2,1024]{3,2,1,0:T(2,128)S(1)} %fusion.13), channel_id=1, source_target_pairs={{0,16},{16,0},{8,24},{24,8},{32,48},{48,32},{40,56},{56,40},{64,80... | collective-permute-start | bytes 786440 | tf_op jit(solution)/shard_map/ppermute | solution.py:33
  140.5 0.1 fusion.34
  140.7 5.5 %collective-permute-done.5 = f32[4,8,2,1024]{3,2,1,0:T(2,128)S(1)} collective-permute-done((f32[4,8,2,1024]{3,2,1,0:T(2,128)S(1)}, f32[4,8,2,1024]{3,2,1,0:T(2,128)S(1)}, u32[]{:S(2)}, u32[]{:S(2)}) %collective-permute-start.5) | collective-permute-done | bytes 262176 | tf_op jit(solution)/shard_map/ppermute | solution.py:33
  146.2 0.3 broadcast_select_fusion.8
  146.5 0.1 fusion.14
  146.7 0.1 pad_maximum_fusion.6
  146.8 0.1 fusion.18
  146.9 3.9 %collective-permute-start.6 = (f32[4,4,2,1024]{3,2,1,0:T(2,128)S(1)}, f32[4,4,2,1024]{3,2,1,0:T(2,128)S(1)}, u32[]{:S(2)}, u32[]{:S(2)}) collective-permute-start(f32[4,4,2,1024]{3,2,1,0:T(2,128)S(1)} %fusion.18), channel_id=1, source_target_pairs={{0,32},{32,0},{8,40},{40,8},{16,48},{48,16},{24,56},{56,24},{64,96... | collective-permute-start | bytes 393224 | tf_op jit(solution)/shard_map/ppermute | solution.py:33
  150.8 0.1 fusion.31
  151.0 2.7 %collective-permute-done.6 = f32[4,4,2,1024]{3,2,1,0:T(2,128)S(1)} collective-permute-done((f32[4,4,2,1024]{3,2,1,0:T(2,128)S(1)}, f32[4,4,2,1024]{3,2,1,0:T(2,128)S(1)}, u32[]{:S(2)}, u32[]{:S(2)}) %collective-permute-start.6) | collective-permute-done | bytes 131104 | tf_op jit(solution)/shard_map/ppermute | solution.py:33
  153.8 0.1 broadcast_select_fusion.12
  153.9 0.1 fusion.19
  154.0 0.1 pad_maximum_fusion.7
  154.1 3.5 %collective-permute-start.7 = (f32[4,2,2,1024]{3,2,1,0:T(2,128)S(1)}, f32[4,2,2,1024]{3,2,1,0:T(2,128)S(1)}, u32[]{:S(2)}, u32[]{:S(2)}) collective-permute-start(f32[4,2,2,1024]{3,2,1,0:T(2,128)S(1)} %fusion.21), channel_id=1, source_target_pairs={{0,64},{64,0},{8,72},{72,8},{16,80},{80,16},{24,88},{88,24},{32,96... | collective-permute-start | bytes 196616 | tf_op jit(solution)/shard_map/ppermute | solution.py:33
  157.7 2.2 %collective-permute-done.7 = f32[4,2,2,1024]{3,2,1,0:T(2,128)S(1)} collective-permute-done((f32[4,2,2,1024]{3,2,1,0:T(2,128)S(1)}, f32[4,2,2,1024]{3,2,1,0:T(2,128)S(1)}, u32[]{:S(2)}, u32[]{:S(2)}) %collective-permute-start.7) | collective-permute-done | bytes 65568 | tf_op jit(solution)/shard_map/ppermute | solution.py:33
  159.8 0.1 broadcast_select_fusion.16
  160.0 8.6 %collective-permute-start.8 = (f32[4,1,2,1024]{3,2,0,1:T(2,128)S(1)}, f32[4,1,2,1024]{3,2,0,1:T(2,128)S(1)}, u32[]{:S(2)}, u32[]{:S(2)}) collective-permute-start(f32[4,1,2,1024]{3,2,0,1:T(2,128)S(1)} %fusion.24), channel_id=1, source_target_pairs={{0,128},{128,0},{8,136},{136,8},{16,144},{144,16},{24,152},{152,24... | collective-permute-start | bytes 98312 | tf_op jit(solution)/shard_map/ppermute | solution.py:33
  168.7 1.9 %collective-permute-done.8 = f32[4,1,2,1024]{3,2,0,1:T(2,128)S(1)} collective-permute-done((f32[4,1,2,1024]{3,2,0,1:T(2,128)S(1)}, f32[4,1,2,1024]{3,2,0,1:T(2,128)S(1)}, u32[]{:S(2)}, u32[]{:S(2)}) %collective-permute-start.8) | collective-permute-done | bytes 32800 | tf_op jit(solution)/shard_map/ppermute | solution.py:33
  170.6 0.6 pad_maximum_fusion.8
  (41 shorter events, 0.6 us)
Async XLA Ops:
  0.0 8.6 %copy-start.9 = (bf16[4,256]{1,0:T(4,128)(2,1)S(1)}, bf16[4,256]{1,0:T(4,128)(2,1)}, u32[]{:S(2)}) copy-start(bf16[4,256]{1,0:T(4,128)(2,1)} %param.8) | copy-start | bytes 6148
  1.9 97.8 %collective-permute-start = (f32[1,64,1024]{2,1,0:T(8,128)}, f32[1,64,1024]{2,1,0:T(8,128)S(1)}, u32[]{:S(2)}, u32[]{:S(2)}) collective-permute-start(f32[1,64,1024]{2,1,0:T(8,128)} %get-tuple-element.69), channel_id=1, source_target_pairs={{0,8},{8,16},{16,24},{24,32},{32,40},{40,48},{48,56},{56,64},{64,7... | collective-permute-start | bytes 786440 | tf_op jit(solution)/shard_map/ppermute | solution.py:18
  5.4 94.4 %collective-permute-start.1 = (f32[1,64,1024]{2,1,0:T(8,128)}, f32[1,64,1024]{2,1,0:T(8,128)}, u32[]{:S(2)}, u32[]{:S(2)}) collective-permute-start(f32[1,64,1024]{2,1,0:T(8,128)} %get-tuple-element.68), channel_id=1, source_target_pairs={{8,0},{16,8},{24,16},{32,24},{40,32},{48,40},{56,48},{64,56},{72,6... | collective-permute-start | bytes 786440 | tf_op jit(solution)/shard_map/ppermute | solution.py:21
  95.5 2.5 %copy-start = (f32[4,64,1024]{2,1,0:T(8,128)S(1)}, f32[4,64,1024]{2,1,0:T(8,128)}, u32[]{:S(2)}) copy-start(f32[4,64,1024]{2,1,0:T(8,128)} %param.6) | copy-start | bytes 3145732
  98.9 9.5 %copy-start.8 = (s32[64,1024]{1,0:T(8,128)S(1)}, s32[64,1024]{1,0:T(8,128)}, u32[]{:S(2)}) copy-start(s32[64,1024]{1,0:T(8,128)} %param.9) | copy-start | bytes 786436
  99.7 10.3 %copy-start.6 = (f32[1,64,1024]{2,1,0:T(8,128)}, f32[1,64,1024]{2,1,0:T(8,128)S(1)}, u32[]{:S(2)}) copy-start(f32[1,64,1024]{2,1,0:T(8,128)S(1)} %collective-permute-done) | copy-start | bytes 786436
  100.8 1.2 copy-start.1
  102.6 10.5 %collective-permute-start.2 = (f32[6,1,1024]{2,1,0:T(1,128)}, f32[6,1,1024]{2,1,0:T(1,128)}, u32[]{:S(2)}, u32[]{:S(2)}) collective-permute-start(f32[6,1,1024]{2,1,0:T(1,128)} %get-tuple-element.64), channel_id=1, source_target_pairs={{0,1},{1,2},{2,3},{3,4},{4,5},{5,6},{6,7},{8,9},{9,10},{10,11},{11... | collective-permute-start | bytes 73736 | tf_op jit(solution)/shard_map/ppermute | solution.py:18
  104.6 8.6 %collective-permute-start.3 = (f32[6,1,1024]{2,1,0:T(1,128)}, f32[6,1,1024]{2,1,0:T(1,128)}, u32[]{:S(2)}, u32[]{:S(2)}) collective-permute-start(f32[6,1,1024]{2,1,0:T(1,128)} %get-tuple-element.63), channel_id=1, source_target_pairs={{1,0},{2,1},{3,2},{4,3},{5,4},{6,5},{7,6},{9,8},{10,9},{11,10},{12... | collective-permute-start | bytes 73736 | tf_op jit(solution)/shard_map/ppermute | solution.py:21
  111.1 2.0 %copy-start.2 = (f32[6,64,1024]{2,1,0:T(8,128)S(1)}, f32[6,64,1024]{2,1,0:T(8,128)}, u32[]{:S(2)}) copy-start(f32[6,64,1024]{2,1,0:T(8,128)} %copy-done.1) | copy-start | bytes 4718596
  113.1 1.6 copy-start.5
  113.1 1.6 copy-start.7
  114.7 3.3 %copy-start.3 = (f32[1,4,64,1024]{3,2,1,0:T(8,128)S(1)}, f32[1,4,64,1024]{3,2,1,0:T(8,128)}, u32[]{:S(2)}) copy-start(f32[1,4,64,1024]{3,2,1,0:T(8,128)} %get-tuple-element.92) | copy-start | bytes 3145732
  114.7 3.3 %copy-start.4 = (f32[1,4,64,1024]{3,2,1,0:T(8,128)S(1)}, f32[1,4,64,1024]{3,2,1,0:T(8,128)}, u32[]{:S(2)}) copy-start(f32[1,4,64,1024]{3,2,1,0:T(8,128)} %get-tuple-element.93) | copy-start | bytes 3145732
  120.9 14.7 %collective-permute-start.4 = (f32[4,16,2,1024]{3,2,1,0:T(2,128)S(1)}, f32[4,16,2,1024]{3,2,1,0:T(2,128)S(1)}, u32[]{:S(2)}, u32[]{:S(2)}) collective-permute-start(f32[4,16,2,1024]{3,2,1,0:T(2,128)S(1)} %fusion.10), channel_id=1, source_target_pairs={{0,8},{8,0},{16,24},{24,16},{32,40},{40,32},{48,56},{56,48},{64,72... | collective-permute-start | bytes 1572872 | tf_op jit(solution)/shard_map/ppermute | solution.py:33
  137.1 9.1 %collective-permute-start.5 = (f32[4,8,2,1024]{3,2,1,0:T(2,128)S(1)}, f32[4,8,2,1024]{3,2,1,0:T(2,128)S(1)}, u32[]{:S(2)}, u32[]{:S(2)}) collective-permute-start(f32[4,8,2,1024]{3,2,1,0:T(2,128)S(1)} %fusion.13), channel_id=1, source_target_pairs={{0,16},{16,0},{8,24},{24,8},{32,48},{48,32},{40,56},{56,40},{64,80... | collective-permute-start | bytes 786440 | tf_op jit(solution)/shard_map/ppermute | solution.py:33
  146.9 6.9 %collective-permute-start.6 = (f32[4,4,2,1024]{3,2,1,0:T(2,128)S(1)}, f32[4,4,2,1024]{3,2,1,0:T(2,128)S(1)}, u32[]{:S(2)}, u32[]{:S(2)}) collective-permute-start(f32[4,4,2,1024]{3,2,1,0:T(2,128)S(1)} %fusion.18), channel_id=1, source_target_pairs={{0,32},{32,0},{8,40},{40,8},{16,48},{48,16},{24,56},{56,24},{64,96... | collective-permute-start | bytes 393224 | tf_op jit(solution)/shard_map/ppermute | solution.py:33
  154.1 5.7 %collective-permute-start.7 = (f32[4,2,2,1024]{3,2,1,0:T(2,128)S(1)}, f32[4,2,2,1024]{3,2,1,0:T(2,128)S(1)}, u32[]{:S(2)}, u32[]{:S(2)}) collective-permute-start(f32[4,2,2,1024]{3,2,1,0:T(2,128)S(1)} %fusion.21), channel_id=1, source_target_pairs={{0,64},{64,0},{8,72},{72,8},{16,80},{80,16},{24,88},{88,24},{32,96... | collective-permute-start | bytes 196616 | tf_op jit(solution)/shard_map/ppermute | solution.py:33
  160.0 10.5 %collective-permute-start.8 = (f32[4,1,2,1024]{3,2,0,1:T(2,128)S(1)}, f32[4,1,2,1024]{3,2,0,1:T(2,128)S(1)}, u32[]{:S(2)}, u32[]{:S(2)}) collective-permute-start(f32[4,1,2,1024]{3,2,0,1:T(2,128)S(1)} %fusion.24), channel_id=1, source_target_pairs={{0,128},{128,0},{8,136},{136,8},{16,144},{144,16},{24,152},{152,24... | collective-permute-start | bytes 98312 | tf_op jit(solution)/shard_map/ppermute | solution.py:33
where the time goes:
time: 172 us; the launch traced here: 171 us
  matrix products  66.4 us (39%)
  local copies, waits for them, and re-layouts  34.8 us (20%)
  starting transfers between devices  32.7 us (19%)
  waiting for transfers between devices  24 us (14%)
  other arithmetic  12.7 us (7%)
    dot_general x4, matrix products, lookup(): lax.dot_general(transfer, one_hot, (((1,), (1,)), ((), ())), preferred_el...  66.4 us
    ppermute x5, waiting for transfers between devices, from_partner(): return lax.ppermute(block, axis, route)  24 us
    ppermute x5, starting transfers between devices, from_partner(): return lax.ppermute(block, axis, route)  22.2 us
    slice x1, local copies, waits for them, and re-layouts, shards(): looked_up[:, k, :].reshape(brick_shape)  19.5 us
    ppermute x2, starting transfers between devices, with_halo(): lax.ppermute(lax.slice_in_dim(block, block.shape[dim] - width, None, axis...  5.39 us
    unnamed x24, local copies, waits for them, and re-layouts  5.14 us
    ppermute x2, starting transfers between devices, with_halo(): lax.ppermute(lax.slice_in_dim(block, 0, width, axis=dim), axis, backward)  5.12 us
  transfers between devices with their start and end apart: 9, of which 5 were waited for; matrix products, arithmetic and copies ran while one was open for 57% of the time, Pallas kernels for 0%

commit v1 on v0

v1 whole, which is shorter than its diff:
```python
import jax
import jax.numpy as jnp
from jax import lax
from jax.experimental import pallas as pl
from jax.experimental.pallas import tpu as pltpu
from jax.sharding import PartitionSpec as P

LIGHT_X = 0.48
LIGHT_Y = 0.6
LIGHT_Z = 0.64
UNIT = 2048.0
LANES = 128
VMEM_LIMIT = 48 * 1024 * 1024
F32 = jnp.float32


def params():
    return pltpu.CompilerParams(vmem_limit_bytes=VMEM_LIMIT)


def faces_kernel(d_ref, za_ref, zb_ref, ya_ref, yb_ref, low, high, sems):
    depth, rows = d_ref.shape[0], d_ref.shape[1]
    slab_odd = lax.axis_index("slab") & 1
    lat_odd = lax.axis_index("lat") & 1
    last = depth - 1
    copies = [
        pltpu.make_async_copy(d_ref.at[:, pl.ds(0, 8)], low, sems.at[0]),
        pltpu.make_async_copy(d_ref.at[:, pl.ds(rows - 8, 8)], high, sems.at[1]),
        pltpu.make_async_copy(d_ref.at[last - last * slab_odd], za_ref, sems.at[2]),
        pltpu.make_async_copy(d_ref.at[last * slab_odd], zb_ref, sems.at[3]),
    ]
    for copy in copies:
        copy.start()
    copies[0].wait()
    copies[1].wait()
    odd = lat_odd == 1
    for k in range(depth):
        first, final = low[k, 0:1], high[k, 7:8]
        ya_ref[k : k + 1, :] = jnp.where(odd, first, final)
        yb_ref[k : k + 1, :] = jnp.where(odd, final, first)
    copies[2].wait()
    copies[3].wait()


def faces(density):
    depth, rows, line = density.shape
    return pl.pallas_call(
        faces_kernel,
        out_shape=[
            jax.ShapeDtypeStruct((rows, line), F32),
            jax.ShapeDtypeStruct((rows, line), F32),
            jax.ShapeDtypeStruct((depth, line), F32),
            jax.ShapeDtypeStruct((depth, line), F32),
        ],
        in_specs=[pl.BlockSpec(memory_space=pl.ANY)],
        out_specs=[pl.BlockSpec(memory_space=pl.ANY)] * 2
        + [pl.BlockSpec(memory_space=pltpu.VMEM)] * 2,
        scratch_shapes=[
            pltpu.VMEM((depth, 8, line), F32),
            pltpu.VMEM((depth, 8, line), F32),
            pltpu.SemaphoreType.DMA((4,)),
        ],
        compiler_params=params(),
        name="faces",
    )(density)


def look_up(table, bins):
    column = bins & (LANES - 1)
    upper = bins >= LANES
    words = []
    for low_half, high_half in table:
        a = jnp.take_along_axis(low_half, column, axis=1, mode="promise_in_bounds")
        b = jnp.take_along_axis(high_half, column, axis=1, mode="promise_in_bounds")
        words.append(jnp.where(upper, b, a))
    values = []
    for word in words:
        values += [(word & 0xFFFF).astype(F32), (word >> 16).astype(F32)]
    return values


def packed_table(t_ref):
    units = (t_ref[...].astype(F32) * UNIT).astype(jnp.int32)
    table = []
    for pair in range(2):
        word = units[2 * pair : 2 * pair + 1] | (units[2 * pair + 1 : 2 * pair + 2] << 16)
        table.append(
            [jnp.broadcast_to(word[:, h * LANES : (h + 1) * LANES], (8, LANES)) for h in range(2)]
        )
    return table


def cells_kernel(
    spacing, d_hbm, b_ref, t_ref, o_ref, ya_ref, yb_ref, c_ref, w_ref, a_ref, n_ref, d, sem
):
    depth, rows, line = d_hbm.shape
    chunks = line // LANES
    copy = pltpu.make_async_copy(d_hbm, d.at[:, pl.ds(8, rows)], sem)
    copy.start()
    lat = lax.axis_index("lat")
    lat_odd = (lat & 1) == 1
    keep_low = jnp.where(lat == 0, 0.0, 1.0).astype(F32)
    keep_high = jnp.where(lat == lax.axis_size("lat") - 1, 0.0, 1.0).astype(F32)
    table = packed_table(t_ref)
    for k in range(depth):
        from_a, from_b = ya_ref[k : k + 1, :], yb_ref[k : k + 1, :]
        d[k, 7:8, :] = jnp.where(lat_odd, from_a, from_b) * keep_low
        d[k, rows + 8 : rows + 9, :] = jnp.where(lat_odd, from_b, from_a) * keep_high
    lane = lax.broadcasted_iota(jnp.int32, (8, LANES), 1)
    sub = lax.broadcasted_iota(jnp.int32, (8, LANES), 0)
    first_lane, last_lane = lane == 0, lane == LANES - 1
    first_sub, last_sub = sub == 0, sub == 7
    scale = spacing / UNIT
    copy.wait()

    def tile(t, carry):
        base = pl.multiple_of(t * 8, 8)
        for c in range(chunks):
            cols = slice(c * LANES, (c + 1) * LANES)

            def cell(k, row, column=c):
                return d[k, pl.ds(row, 8), column * LANES : (column + 1) * LANES]

            reverse = o_ref[pl.ds(base, 8), cols] == 1
            passed, colors, tilt, norm = [], [], [], []
            for k in range(depth):
                here = cell(k, base + 8)
                before, after = cell(k, base), cell(k, base + 16)
                left = cell(k, base + 8, c - 1) if c > 0 else jnp.zeros_like(here)
                right = cell(k, base + 8, c + 1) if c < chunks - 1 else jnp.zeros_like(here)
                step_x = pltpu.roll(jnp.where(first_lane, right, here), LANES - 1, 1) - pltpu.roll(
                    jnp.where(last_lane, left, here), 1, 1
                )
                step_y = pltpu.roll(jnp.where(first_sub, after, here), 7, 0) - pltpu.roll(
                    jnp.where(last_sub, before, here), 1, 0
                )
                tilt.append(LIGHT_X * step_x + LIGHT_Y * step_y)
                norm.append(step_x * step_x + step_y * step_y + 1.0)
                red, green, blue, extinction = look_up(table, b_ref[k, pl.ds(base, 8), cols])
                passed.append(jnp.exp(-(extinction * scale * here)))
                colors.append((red, green, blue))
            t0, t1, t2, t3 = passed
            front, back = t0 * t1, t2 * t3
            ahead = [
                jnp.where(reverse, t1 * back, 1.0),
                jnp.where(reverse, back, t0),
                jnp.where(reverse, t3, front),
                jnp.where(reverse, 1.0, front * t2),
            ]
            total = [None, None, None]
            for k in range(depth):
                weight = (1.0 - passed[k]) * (1.0 / UNIT) * ahead[k]
                if k in (0, depth - 1):
                    edge = 0 if k == 0 else 1
                    for i in range(3):
                        w_ref[edge, i, pl.ds(base, 8), cols] = colors[k][i] * weight
                    a_ref[edge, pl.ds(base, 8), cols] = tilt[k]
                    n_ref[edge, pl.ds(base, 8), cols] = norm[k]
                    continue
                step_z = cell(k + 1, base + 8) - cell(k - 1, base + 8)
                shade = (tilt[k] + LIGHT_Z * step_z) * lax.rsqrt(norm[k] + step_z * step_z)
                weight = weight + weight * shade
                for i in range(3):
                    term = colors[k][i] * weight
                    total[i] = term if total[i] is None else total[i] + term
            for i in range(3):
                c_ref[i, pl.ds(base, 8), cols] = total[i]
            c_ref[3, pl.ds(base, 8), cols] = front * back
        return carry

    lax.fori_loop(0, rows // 8, tile, 0)


def cells(density, bins, transfer, order, ya, yb, spacing):
    depth, rows, line = density.shape
    vmem = pl.BlockSpec(memory_space=pltpu.VMEM)
    return pl.pallas_call(
        lambda *refs: cells_kernel(spacing, *refs),
        out_shape=[
            jax.ShapeDtypeStruct((4, rows, line), F32),
            jax.ShapeDtypeStruct((2, 3, rows, line), F32),
            jax.ShapeDtypeStruct((2, rows, line), F32),
            jax.ShapeDtypeStruct((2, rows, line), F32),
        ],
        in_specs=[pl.BlockSpec(memory_space=pl.ANY)] + [vmem] * 5,
        out_specs=[vmem] * 4,
        scratch_shapes=[pltpu.VMEM((depth, rows + 16, line), F32), pltpu.SemaphoreType.DMA],
        compiler_params=params(),
        cost_estimate=pl.CostEstimate(
            flops=100 * depth * rows * line, bytes_accessed=12 * depth * rows * line, transcendentals=2 * depth * rows * line
        ),
        name="cells",
    )(density, bins, transfer, order, ya, yb)


def swap_pieces(tiles, sub):
    for size in (4, 2):
        keep = (sub & size) == 0
        step = size // 2
        result = list(tiles)
        for i in range(4):
            if i & step == 0:
                a, b = tiles[i], tiles[i | step]
                result[i] = jnp.where(keep, a, pltpu.roll(b, size, 0))
                result[i | step] = jnp.where(keep, pltpu.roll(a, 8 - size, 0), b)
        tiles = result
    return tiles


def edges_kernel(d_ref, za_ref, zb_ref, o_ref, c_ref, w_ref, a_ref, n_ref, *rest):
    outs, mask_ref, s = rest[:8], rest[8], rest[9]
    depth, rows, line = d_ref.shape
    slab = lax.axis_index("slab")
    slab_odd = (slab & 1) == 1
    keep_low = jnp.where(slab == 0, 0.0, 1.0).astype(F32)
    keep_high = jnp.where(slab == lax.axis_size("slab") - 1, 0.0, 1.0).astype(F32)
    sub = lax.broadcasted_iota(jnp.int32, (8, LANES), 0)
    chunks = line // LANES

    def part(index, carry):
        half, c = index // chunks, index % chunks
        cols = pl.ds(pl.multiple_of(c * LANES, LANES), LANES)
        channels = [[] for _ in range(5)]
        for quarter in range(4):
            at = pl.ds(pl.multiple_of(16 * quarter + 8 * half, 8), 8)
            from_a, from_b = za_ref[at, cols], zb_ref[at, cols]
            below = jnp.where(slab_odd, from_a, from_b) * keep_low
            above = jnp.where(slab_odd, from_b, from_a) * keep_high
            total = [c_ref[i, at, cols] for i in range(3)]
            steps = (d_ref[1, at, cols] - below, above - d_ref[depth - 2, at, cols])
            for edge in range(2):
                step_z = steps[edge]
                shade = 1.0 + (a_ref[edge, at, cols] + LIGHT_Z * step_z) * lax.rsqrt(
                    n_ref[edge, at, cols] + step_z * step_z
                )
                for i in range(3):
                    total[i] = total[i] + w_ref[edge, i, at, cols] * shade
            for i in range(3):
                channels[i].append(total[i])
            channels[3].append(c_ref[3, at, cols])
            channels[4].append(o_ref[at, cols].astype(F32))
        for i in range(5):
            for piece, value in enumerate(swap_pieces(channels[i], sub)):
                s[4 * half + piece, i, :, cols] = value
        return carry

    lax.fori_loop(0, 2 * chunks, part, 0)
    place = slab & 7
    for j in range(8):
        for i in range(4):
            outs[j][i] = s[place ^ j, i]
    mask_ref[...] = s[place, 4]


def edges(density, za, zb, order, color, weight, tilt, norm):
    depth, rows, line = density.shape
    vmem = pl.BlockSpec(memory_space=pltpu.VMEM)
    return pl.pallas_call(
        edges_kernel,
        out_shape=[jax.ShapeDtypeStruct((4, 8, line), F32)] * 8
        + [jax.ShapeDtypeStruct((8, line), F32)],
        in_specs=[vmem] * 8,
        out_specs=[vmem] * 9,
        scratch_shapes=[pltpu.VMEM((8, 5, 8, line), F32)],
        compiler_params=params(),
        cost_estimate=pl.CostEstimate(
            flops=40 * depth * rows * line, bytes_accessed=4 * depth * rows * line, transcendentals=depth * rows * line
        ),
        name="edges",
    )(density, za, zb, order, color, weight, tilt, norm)


def merge(a, b, b_first):
    front = [jnp.where(b_first, y, x) for x, y in zip(a, b)]
    back = [jnp.where(b_first, x, y) for x, y in zip(a, b)]
    return [front[i] + front[3] * back[i] for i in range(3)] + [front[3] * back[3]]


def merge_tree(blocks, mask, place):
    bit = 0
    while len(blocks) > 1:
        b_first = jnp.logical_xor(mask > 0.5, (place >> bit & 1) == 1)
        blocks = [merge(blocks[i], blocks[i + 1], b_first) for i in range(0, len(blocks), 2)]
        bit += 1
    return blocks[0]


def eight_kernel(*refs):
    ins, mask_ref, outs, own_mask = refs[:8], refs[8], refs[9:13], refs[13]
    line = mask_ref.shape[1]
    slab = lax.axis_index("slab")
    place, quarter = slab & 7, slab >> 3
    sub = lax.broadcasted_iota(jnp.int32, (8, LANES), 0) // 2

    def part(c, carry):
        cols = pl.ds(pl.multiple_of(c * LANES, LANES), LANES)
        mask = mask_ref[:, cols]
        blocks = [[ref[i, :, cols] for i in range(4)] for ref in ins]
        merged = merge_tree(blocks, mask, place)
        for j in range(4):
            target = quarter ^ j
            packed = None
            for i in range(4):
                moved = pltpu.roll(merged[i], (2 * i + 8 - 2 * target) & 7, 0)
                packed = moved if packed is None else jnp.where(sub == i, moved, packed)
            outs[j][:, cols] = packed
        own_mask[:, cols] = pltpu.roll(mask, (8 - 2 * quarter) & 7, 0)
        return carry

    lax.fori_loop(0, line // LANES, part, 0)


def merge_eight(blocks, mask):
    line = mask.shape[1]
    vmem = pl.BlockSpec(memory_space=pltpu.VMEM)
    return pl.pallas_call(
        eight_kernel,
        out_shape=[jax.ShapeDtypeStruct((8, line), F32)] * 5,
        in_specs=[vmem] * 9,
        out_specs=[vmem] * 5,
        compiler_params=params(),
        name="merge_eight",
    )(*blocks, mask)


def four_kernel(*refs):
    ins, mask_ref, out = refs[:4], refs[4], refs[5]
    place = lax.axis_index("slab") >> 3
    mask = mask_ref[0:2, :]
    blocks = [[ref[2 * i : 2 * i + 2, :] for i in range(4)] for ref in ins]
    merged = merge_tree(blocks, mask, place)
    for i in range(3):
        out[i] = merged[i]
    out[3] = 1.0 - merged[3]


def merge_four(blocks, mask):
    line = mask.shape[1]
    vmem = pl.BlockSpec(memory_space=pltpu.VMEM)
    return pl.pallas_call(
        four_kernel,
        out_shape=jax.ShapeDtypeStruct((4, 2, line), F32),
        in_specs=[vmem] * 5,
        out_specs=vmem,
        compiler_params=params(),
        name="merge_four",
    )(*blocks, mask)


def swap(block, axis, step):
    count = lax.axis_size(axis)
    return lax.ppermute(block, axis, [(i, i ^ step) for i in range(count)])


def swap_odd(block, axis):
    count = lax.axis_size(axis)
    route = []
    for i in range(1, count, 2):
        route += [(i, (i + 1) % count), ((i + 1) % count, i)]
    return lax.ppermute(block, axis, route)


def shards(density, bins, transfer, depth_order):
    depth_cells = density.shape[0]
    spacing = 1.5 / (depth_cells * lax.axis_size("slab"))
    za, zb, ya, yb = faces(density)
    za, zb = swap(za, "slab", 1), swap_odd(zb, "slab")
    ya, yb = swap(ya, "lat", 1), swap_odd(yb, "lat")
    color, weight, tilt, norm = cells(density, bins, transfer, depth_order, ya, yb, spacing)
    *blocks, mask = edges(density, za, zb, depth_order, color, weight, tilt, norm)
    blocks = [blocks[0]] + [swap(blocks[j], "slab", j) for j in range(1, 8)]
    *quarters, mask = merge_eight(blocks, mask)
    quarters = [quarters[0]] + [swap(quarters[j], "slab", 8 * j) for j in range(1, 4)]
    return merge_four(quarters, mask)


def solution(mesh):
    return jax.shard_map(
        shards,
        mesh=mesh,
        in_specs=(P("slab", "lat", None), P("slab", "lat", None), P(), P("lat", None)),
        out_specs=P(None, ("lat", "slab"), None),
        check_vma=False,
    )
```

time: 172 us -> 55.3 us (0.32)
  matrix products: 66.4 us -> 0 us
  local copies, waits for them, and re-layouts: 34.8 us -> 4.02 us
  other arithmetic: 12.7 us -> 0 us
  Pallas kernels: 0 us -> 7.06 us
  waiting for transfers between devices: 24 us -> 17.1 us
  starting transfers between devices: 32.7 us -> 26.8 us
    dot_general x4 -> x0, matrix products: 66.4 us -> none  [lookup(): lax.dot_general(transfer, one_hot, (((1,), (1,)), ((), ())), preferred_el...]
    slice x4 -> x0, local copies, waits for them, and re-layouts: 22.1 us -> none  [the longest x1 19.5 us: shards(): looked_up[:, k, :].reshape(brick_shape)]
    pallas_call x0 -> x5, Pallas kernels: none -> 7.06 us  [the longest x1 3.56 us: cells(): pl.pallas_call(lambda *refs: cells_kernel(spacing, *refs), out_shape=[jax...]
    ppermute x9 -> x14, waiting for transfers between devices: 24 us -> 17.1 us  [the longest x12 15.2 us: swap(): return lax.ppermute(block, axis, [(i, i ^ step) for i in range(count)])]
    ppermute x9 -> x14, starting transfers between devices: 32.7 us -> 26.8 us  [the longest x12 18.7 us: swap(): return lax.ppermute(block, axis, [(i, i ^ step) for i in range(count)])]
    another operation x2 -> x0, local copies, waits for them, and re-layouts: 3.49 us -> none  [the longest x1 2.53 us: shards(): jnp.stack([looked_up[:, k, :].reshape(brick_shape) for k in range(3)], ax...]
    mul x6 -> x0, other arithmetic: 3.49 us -> none  [the longest x1 3.3 us: shards(): radiance = emission * (shading * (1.0 - jnp.exp(-optical)))[None]]
    select_n x16 -> x0, other arithmetic: 2.93 us -> none  [the longest x5 1.25 us: shards(): in_front = jnp.where(masks[None], upper_half, lower_half)]
  transfers between devices with their start and end apart: 9 -> 14, of which waited for: 5 -> 9; matrix products, arithmetic and copies ran while one was open for 57% -> 0% of each run, Pallas kernels for 0% -> 6%
where the time goes in v1:
time: 55.3 us; the launch traced here: 55.1 us
  starting transfers between devices  26.8 us (48%)
  waiting for transfers between devices  17.1 us (31%)
  Pallas kernels  7.06 us (13%)
  local copies, waits for them, and re-layouts  4.02 us (7%)
    ppermute x12, starting transfers between devices, swap(): return lax.ppermute(block, axis, [(i, i ^ step) for i in range(count)])  18.7 us
    ppermute x12, waiting for transfers between devices, swap(): return lax.ppermute(block, axis, [(i, i ^ step) for i in range(count)])  15.2 us
    ppermute x2, starting transfers between devices, swap_odd(): return lax.ppermute(block, axis, route)  8.12 us
    unnamed x12, local copies, waits for them, and re-layouts  4.02 us
    pallas_call x1, Pallas kernels, cells(): pl.pallas_call(lambda *refs: cells_kernel(spacing, *refs), out_shape=[jax...  3.56 us
    pallas_call x1, Pallas kernels, edges(): pl.pallas_call(edges_kernel, out_shape=[jax.ShapeDtypeStruct((4, 8, line)...  2.38 us
    ppermute x2, waiting for transfers between devices, swap_odd(): return lax.ppermute(block, axis, route)  1.99 us
  transfers between devices with their start and end apart: 14, of which 9 were waited for; matrix products, arithmetic and copies ran while one was open for 0% of the time, Pallas kernels for 6%

profile of v1, /device:TPU:2, one launch (start us, length us, event | category | flops | bytes accessed | tf_op | source)
XLA Modules:
  0.0 55.1 jit_solution(4339280721315195661)
XLA Ops:
  0.0 0.0 copy-start
  0.0 1.2 %copy-done = f32[4,64,1024]{2,1,0:T(8,128)S(1)} copy-done((f32[4,64,1024]{2,1,0:T(8,128)S(1)}, f32[4,64,1024]{2,1,0:T(8,128)}, u32[]{:S(2)}) %copy-start) | copy-done | bytes 1048600
  1.2 0.0 copy-start.2
  1.2 0.2 faces.1
  1.4 1.7 %collective-permute-start = (f32[64,1024]{1,0:T(8,128)S(1)}, f32[64,1024]{1,0:T(8,128)S(1)}, u32[]{:S(2)}, u32[]{:S(2)}) collective-permute-start(f32[64,1024]{1,0:T(8,128)S(1)} %get-tuple-element.27), channel_id=1, source_target_pairs={{0,8},{8,0},{16,24},{24,16},{32,40},{40,32},{48,56},{56,48},{64,72... | collective-permute-start | bytes 786440 | tf_op jit(solution)/shard_map/ppermute | solution.py:352
  3.1 7.5 %collective-permute-start.1 = (f32[64,1024]{1,0:T(8,128)S(1)}, f32[64,1024]{1,0:T(8,128)S(1)}, u32[]{:S(2)}, u32[]{:S(2)}) collective-permute-start(f32[64,1024]{1,0:T(8,128)S(1)} %get-tuple-element.28), channel_id=1, source_target_pairs={{8,16},{16,8},{24,32},{32,24},{40,48},{48,40},{56,64},{64,56},{72,... | collective-permute-start | bytes 786440 | tf_op jit(solution)/shard_map/ppermute | solution.py:360
  10.5 0.0 collective-permute-start.2
  10.5 0.6 %collective-permute-start.3 = (f32[4,1024]{1,0:T(4,128)S(1)}, f32[4,1024]{1,0:T(4,128)S(1)}, u32[]{:S(2)}, u32[]{:S(2)}) collective-permute-start(f32[4,1024]{1,0:T(4,128)S(1)} %get-tuple-element.30), channel_id=1, source_target_pairs={{1,2},{2,1},{3,4},{4,3},{5,6},{6,5},{7,0},{0,7},{9,10},{10,9},{11,... | collective-permute-start | bytes 49160 | tf_op jit(solution)/shard_map/ppermute | solution.py:360
  11.2 0.5 collective-permute-done.2.refs_4_
  11.7 2.0 %collective-permute-done.3.refs_5_ = f32[4,1024]{1,0:T(4,128)S(1)} collective-permute-done((f32[4,1024]{1,0:T(4,128)S(1)}, f32[4,1024]{1,0:T(4,128)S(1)}, u32[]{:S(2)}, u32[]{:S(2)}) %collective-permute-start.3) | collective-permute-done | bytes 16416 | tf_op jit(solution)/shard_map/ppermute | solution.py:360
  13.7 0.0 copy-done.2
  13.7 0.0 copy-start.3
  13.7 0.9 %copy-done.3 = s32[64,1024]{1,0:T(8,128)S(1)} copy-done((s32[64,1024]{1,0:T(8,128)S(1)}, s32[64,1024]{1,0:T(8,128)}, u32[]{:S(2)}) %copy-start.3) | copy-done | bytes 262168
  14.7 0.0 copy-start.5
  14.7 0.7 %copy-done.5 = bf16[4,256]{1,0:T(4,128)(2,1)S(1)} copy-done((bf16[4,256]{1,0:T(4,128)(2,1)S(1)}, bf16[4,256]{1,0:T(4,128)(2,1)}, u32[]{:S(2)}) %copy-start.5) | copy-done | bytes 2072
  15.3 0.0 copy-start.4
  15.3 3.6 %cells.1 = (f32[4,64,1024]{2,1,0:T(8,128)S(1)}, f32[2,3,64,1024]{3,2,1,0:T(8,128)S(1)}, f32[2,64,1024]{2,1,0:T(8,128)S(1)}, f32[2,64,1024]{2,1,0:T(8,128)S(1)}) custom-call(f32[4,64,1024]{2,1,0:T(8,128)S(1)} %copy-done, s32[4,64,1024]{2,1,0:T(8,128)S(1)} %copy-done.2, bf16[4,256]{1,0:T(4,128)(2,1)S(1)} %copy-done.5, s32[64,1024]{1,0:T(8,128)S(1)} %copy-done.3, ...), custom_call_target="tpu_custom_call" | custom-call | flops 26214400 | bytes 3145728 | tf_op jit(solution)/shard_map/cells/pallas_call | solution.py:177
  18.9 0.0 copy-start.1
  18.9 1.2 %copy-done.1 = f32[2,3,64,1024]{3,2,1,0:T(8,128)} copy-done((f32[2,3,64,1024]{3,2,1,0:T(8,128)}, f32[2,3,64,1024]{3,2,1,0:T(8,128)S(1)}, u32[]{:S(2)}) %copy-start.1) | copy-done | bytes 1572888
  20.1 0.0 collective-permute-done.za_ref
  20.1 0.0 collective-permute-done.1.zb_ref
  20.1 0.0 copy-done.4
  20.1 2.4 %edges.1 = (f32[4,8,1024]{2,1,0:T(8,128)S(1)}, f32[4,8,1024]{2,1,0:T(8,128)S(1)}, f32[4,8,1024]{2,1,0:T(8,128)S(1)}, f32[4,8,1024]{2,1,0:T(8,128)S(1)}, f32[4,8,...) custom-call(f32[4,64,1024]{2,1,0:T(8,128)S(1)} %copy-done, ...), custom_call_target="tpu_custom_call" | custom-call | flops 10485760 | bytes 1048576 | tf_op jit(solution)/shard_map/edges/pallas_call | solution.py:258
  22.5 0.1 collective-permute-start.4
  22.6 0.1 collective-permute-start.5
  22.7 4.6 %collective-permute-start.6 = (f32[4,8,1024]{2,1,0:T(8,128)S(1)}, f32[4,8,1024]{2,1,0:T(8,128)S(1)}, u32[]{:S(2)}, u32[]{:S(2)}) collective-permute-start(f32[4,8,1024]{2,1,0:T(8,128)S(1)} %get-tuple-element.38), channel_id=1, source_target_pairs={{0,24},{8,16},{16,8},{24,0},{32,56},{40,48},{48,40},{56,32},{64,88... | collective-permute-start | bytes 393224 | tf_op jit(solution)/shard_map/ppermute | solution.py:352
  27.3 0.0 collective-permute-start.7
  27.3 0.3 collective-permute-start.8
  27.6 1.3 %collective-permute-done.4.refs_1_ = f32[4,8,1024]{2,1,0:T(8,128)S(1)} collective-permute-done((f32[4,8,1024]{2,1,0:T(8,128)S(1)}, f32[4,8,1024]{2,1,0:T(8,128)S(1)}, u32[]{:S(2)}, u32[]{:S(2)}) %collective-permute-start.4) | collective-permute-done | bytes 131104 | tf_op jit(solution)/shard_map/ppermute | solution.py:352
  28.9 0.7 %collective-permute-start.9 = (f32[4,8,1024]{2,1,0:T(8,128)S(1)}, f32[4,8,1024]{2,1,0:T(8,128)S(1)}, u32[]{:S(2)}, u32[]{:S(2)}) collective-permute-start(f32[4,8,1024]{2,1,0:T(8,128)S(1)} %get-tuple-element.41), channel_id=1, source_target_pairs={{0,48},{8,56},{16,32},{24,40},{32,16},{40,24},{48,0},{56,8},{64,11... | collective-permute-start | bytes 393224 | tf_op jit(solution)/shard_map/ppermute | solution.py:352
  29.6 0.8 %collective-permute-done.5.refs_2_ = f32[4,8,1024]{2,1,0:T(8,128)S(1)} collective-permute-done((f32[4,8,1024]{2,1,0:T(8,128)S(1)}, f32[4,8,1024]{2,1,0:T(8,128)S(1)}, u32[]{:S(2)}, u32[]{:S(2)}) %collective-permute-start.5) | collective-permute-done | bytes 131104 | tf_op jit(solution)/shard_map/ppermute | solution.py:352
  30.5 3.9 %collective-permute-start.10 = (f32[4,8,1024]{2,1,0:T(8,128)S(1)}, f32[4,8,1024]{2,1,0:T(8,128)S(1)}, u32[]{:S(2)}, u32[]{:S(2)}) collective-permute-start(f32[4,8,1024]{2,1,0:T(8,128)S(1)} %get-tuple-element.42), channel_id=1, source_target_pairs={{0,56},{8,48},{16,40},{24,32},{32,24},{40,16},{48,8},{56,0},{64,12... | collective-permute-start | bytes 393224 | tf_op jit(solution)/shard_map/ppermute | solution.py:352
  34.3 0.0 collective-permute-done.6.refs_3_
  34.3 0.0 collective-permute-done.7.refs_4_
  34.3 0.3 collective-permute-done.8.refs_5_
  34.6 3.4 %collective-permute-done.9.refs_6_ = f32[4,8,1024]{2,1,0:T(8,128)S(1)} collective-permute-done((f32[4,8,1024]{2,1,0:T(8,128)S(1)}, f32[4,8,1024]{2,1,0:T(8,128)S(1)}, u32[]{:S(2)}, u32[]{:S(2)}) %collective-permute-start.9) | collective-permute-done | bytes 131104 | tf_op jit(solution)/shard_map/ppermute | solution.py:352
  38.0 2.7 %collective-permute-done.10.refs_7_ = f32[4,8,1024]{2,1,0:T(8,128)S(1)} collective-permute-done((f32[4,8,1024]{2,1,0:T(8,128)S(1)}, f32[4,8,1024]{2,1,0:T(8,128)S(1)}, u32[]{:S(2)}, u32[]{:S(2)}) %collective-permute-start.10) | collective-permute-done | bytes 131104 | tf_op jit(solution)/shard_map/ppermute | solution.py:352
  40.8 0.3 merge_eight.1
  41.0 1.7 %collective-permute-start.11 = (f32[8,1024]{1,0:T(8,128)S(1)}, f32[8,1024]{1,0:T(8,128)S(1)}, u32[]{:S(2)}, u32[]{:S(2)}) collective-permute-start(f32[8,1024]{1,0:T(8,128)S(1)} %get-tuple-element.45), channel_id=1, source_target_pairs={{0,64},{8,72},{16,80},{24,88},{32,96},{40,104},{48,112},{56,120},{... | collective-permute-start | bytes 98312 | tf_op jit(solution)/shard_map/ppermute | solution.py:352
  42.7 5.7 %collective-permute-start.12 = (f32[8,1024]{1,0:T(8,128)S(1)}, f32[8,1024]{1,0:T(8,128)S(1)}, u32[]{:S(2)}, u32[]{:S(2)}) collective-permute-start(f32[8,1024]{1,0:T(8,128)S(1)} %get-tuple-element.46), channel_id=1, source_target_pairs={{0,128},{8,136},{16,144},{24,152},{32,160},{40,168},{48,176},{56,1... | collective-permute-start | bytes 98312 | tf_op jit(solution)/shard_map/ppermute | solution.py:352
  48.4 0.0 collective-permute-start.13
  48.4 0.0 collective-permute-done.11.refs_1_
  48.4 2.2 %collective-permute-done.12.refs_2_ = f32[8,1024]{1,0:T(8,128)S(1)} collective-permute-done((f32[8,1024]{1,0:T(8,128)S(1)}, f32[8,1024]{1,0:T(8,128)S(1)}, u32[]{:S(2)}, u32[]{:S(2)}) %collective-permute-start.12) | collective-permute-done | bytes 32800 | tf_op jit(solution)/shard_map/ppermute | solution.py:352
  50.6 3.8 %collective-permute-done.13.refs_3_ = f32[8,1024]{1,0:T(8,128)S(1)} collective-permute-done((f32[8,1024]{1,0:T(8,128)S(1)}, f32[8,1024]{1,0:T(8,128)S(1)}, u32[]{:S(2)}, u32[]{:S(2)}) %collective-permute-start.13) | collective-permute-done | bytes 32800 | tf_op jit(solution)/shard_map/ppermute | solution.py:352
  54.4 0.7 %merge_four.1 = f32[4,2,1024]{2,1,0:T(2,128)} custom-call(f32[8,1024]{1,0:T(8,128)S(1)} %get-tuple-element.44.refs_0_, f32[8,1024]{1,0:T(8,128)S(1)} %collective-permute-done.11.refs_1_, f32[8,1024]{1,0:T(8,128)S(1)} %collective-permute-done.12.refs_2_, f32[8,1024]{1,0:T(8,128)S(1)} %collective-permute-done.13.refs_3_, f32[8,1024]{1,0:T(8,128)S(1)} %get-tuple-element.48.refs_4_), custom_call_target="tpu_custom_call" | custom-call | tf_op jit(solution)/shard_map/merge_four/pallas_call | solution.py:340
Async XLA Ops:
  0.0 1.2 %copy-start = (f32[4,64,1024]{2,1,0:T(8,128)S(1)}, f32[4,64,1024]{2,1,0:T(8,128)}, u32[]{:S(2)}) copy-start(f32[4,64,1024]{2,1,0:T(8,128)} %d_ref.3) | copy-start | bytes 3145732
  1.2 12.5 %copy-start.2 = (s32[4,64,1024]{2,1,0:T(8,128)S(1)}, s32[4,64,1024]{2,1,0:T(8,128)}, u32[]{:S(2)}) copy-start(s32[4,64,1024]{2,1,0:T(8,128)} %refs_1_.1) | copy-start | bytes 3145732
  1.4 18.7 %collective-permute-start = (f32[64,1024]{1,0:T(8,128)S(1)}, f32[64,1024]{1,0:T(8,128)S(1)}, u32[]{:S(2)}, u32[]{:S(2)}) collective-permute-start(f32[64,1024]{1,0:T(8,128)S(1)} %get-tuple-element.27), channel_id=1, source_target_pairs={{0,8},{8,0},{16,24},{24,16},{32,40},{40,32},{48,56},{56,48},{64,72... | collective-permute-start | bytes 786440 | tf_op jit(solution)/shard_map/ppermute | solution.py:352
  3.1 17.0 %collective-permute-start.1 = (f32[64,1024]{1,0:T(8,128)S(1)}, f32[64,1024]{1,0:T(8,128)S(1)}, u32[]{:S(2)}, u32[]{:S(2)}) collective-permute-start(f32[64,1024]{1,0:T(8,128)S(1)} %get-tuple-element.28), channel_id=1, source_target_pairs={{8,16},{16,8},{24,32},{32,24},{40,48},{48,40},{56,64},{64,56},{72,... | collective-permute-start | bytes 786440 | tf_op jit(solution)/shard_map/ppermute | solution.py:360
  10.5 1.2 %collective-permute-start.2 = (f32[4,1024]{1,0:T(4,128)S(1)}, f32[4,1024]{1,0:T(4,128)S(1)}, u32[]{:S(2)}, u32[]{:S(2)}) collective-permute-start(f32[4,1024]{1,0:T(4,128)S(1)} %get-tuple-element.29), channel_id=1, source_target_pairs={{0,1},{1,0},{2,3},{3,2},{4,5},{5,4},{6,7},{7,6},{8,9},{9,8},{10,11... | collective-permute-start | bytes 49160 | tf_op jit(solution)/shard_map/ppermute | solution.py:352
  10.5 3.2 %collective-permute-start.3 = (f32[4,1024]{1,0:T(4,128)S(1)}, f32[4,1024]{1,0:T(4,128)S(1)}, u32[]{:S(2)}, u32[]{:S(2)}) collective-permute-start(f32[4,1024]{1,0:T(4,128)S(1)} %get-tuple-element.30), channel_id=1, source_target_pairs={{1,2},{2,1},{3,4},{4,3},{5,6},{6,5},{7,0},{0,7},{9,10},{10,9},{11,... | collective-permute-start | bytes 49160 | tf_op jit(solution)/shard_map/ppermute | solution.py:360
  13.7 1.0 %copy-start.3 = (s32[64,1024]{1,0:T(8,128)S(1)}, s32[64,1024]{1,0:T(8,128)}, u32[]{:S(2)}) copy-start(s32[64,1024]{1,0:T(8,128)} %o_ref.1) | copy-start | bytes 786436
  14.7 0.7 %copy-start.5 = (bf16[4,256]{1,0:T(4,128)(2,1)S(1)}, bf16[4,256]{1,0:T(4,128)(2,1)}, u32[]{:S(2)}) copy-start(bf16[4,256]{1,0:T(4,128)(2,1)} %refs_2_.1) | copy-start | bytes 6148
  15.3 4.7 %copy-start.4 = (s32[64,1024]{1,0:T(8,128)S(1)}, s32[64,1024]{1,0:T(8,128)}, u32[]{:S(2)}) copy-start(s32[64,1024]{1,0:T(8,128)} %o_ref.1) | copy-start | bytes 786436
  18.9 1.2 %copy-start.1 = (f32[2,3,64,1024]{3,2,1,0:T(8,128)}, f32[2,3,64,1024]{3,2,1,0:T(8,128)S(1)}, u32[]{:S(2)}) copy-start(f32[2,3,64,1024]{3,2,1,0:T(8,128)S(1)} %get-tuple-element.32.w_ref) | copy-start | bytes 4718596
  22.5 6.5 %collective-permute-start.4 = (f32[4,8,1024]{2,1,0:T(8,128)S(1)}, f32[4,8,1024]{2,1,0:T(8,128)S(1)}, u32[]{:S(2)}, u32[]{:S(2)}) collective-permute-start(f32[4,8,1024]{2,1,0:T(8,128)S(1)} %get-tuple-element.36), channel_id=1, source_target_pairs={{0,8},{8,0},{16,24},{24,16},{32,40},{40,32},{48,56},{56,48},{64,72... | collective-permute-start | bytes 393224 | tf_op jit(solution)/shard_map/ppermute | solution.py:352
  22.6 7.9 %collective-permute-start.5 = (f32[4,8,1024]{2,1,0:T(8,128)S(1)}, f32[4,8,1024]{2,1,0:T(8,128)S(1)}, u32[]{:S(2)}, u32[]{:S(2)}) collective-permute-start(f32[4,8,1024]{2,1,0:T(8,128)S(1)} %get-tuple-element.37), channel_id=1, source_target_pairs={{0,16},{8,24},{16,0},{24,8},{32,48},{40,56},{48,32},{56,40},{64,80... | collective-permute-start | bytes 393224 | tf_op jit(solution)/shard_map/ppermute | solution.py:352
  22.7 11.7 %collective-permute-start.6 = (f32[4,8,1024]{2,1,0:T(8,128)S(1)}, f32[4,8,1024]{2,1,0:T(8,128)S(1)}, u32[]{:S(2)}, u32[]{:S(2)}) collective-permute-start(f32[4,8,1024]{2,1,0:T(8,128)S(1)} %get-tuple-element.38), channel_id=1, source_target_pairs={{0,24},{8,16},{16,8},{24,0},{32,56},{40,48},{48,40},{56,32},{64,88... | collective-permute-start | bytes 393224 | tf_op jit(solution)/shard_map/ppermute | solution.py:352
  27.3 7.1 %collective-permute-start.7 = (f32[4,8,1024]{2,1,0:T(8,128)S(1)}, f32[4,8,1024]{2,1,0:T(8,128)S(1)}, u32[]{:S(2)}, u32[]{:S(2)}) collective-permute-start(f32[4,8,1024]{2,1,0:T(8,128)S(1)} %get-tuple-element.39), channel_id=1, source_target_pairs={{0,32},{8,40},{16,48},{24,56},{32,0},{40,8},{48,16},{56,24},{64,96... | collective-permute-start | bytes 393224 | tf_op jit(solution)/shard_map/ppermute | solution.py:352
  27.3 7.4 %collective-permute-start.8 = (f32[4,8,1024]{2,1,0:T(8,128)S(1)}, f32[4,8,1024]{2,1,0:T(8,128)S(1)}, u32[]{:S(2)}, u32[]{:S(2)}) collective-permute-start(f32[4,8,1024]{2,1,0:T(8,128)S(1)} %get-tuple-element.40), channel_id=1, source_target_pairs={{0,40},{8,32},{16,56},{24,48},{32,8},{40,0},{48,24},{56,16},{64,10... | collective-permute-start | bytes 393224 | tf_op jit(solution)/shard_map/ppermute | solution.py:352
  28.9 9.1 %collective-permute-start.9 = (f32[4,8,1024]{2,1,0:T(8,128)S(1)}, f32[4,8,1024]{2,1,0:T(8,128)S(1)}, u32[]{:S(2)}, u32[]{:S(2)}) collective-permute-start(f32[4,8,1024]{2,1,0:T(8,128)S(1)} %get-tuple-element.41), channel_id=1, source_target_pairs={{0,48},{8,56},{16,32},{24,40},{32,16},{40,24},{48,0},{56,8},{64,11... | collective-permute-start | bytes 393224 | tf_op jit(solution)/shard_map/ppermute | solution.py:352
  30.5 10.3 %collective-permute-start.10 = (f32[4,8,1024]{2,1,0:T(8,128)S(1)}, f32[4,8,1024]{2,1,0:T(8,128)S(1)}, u32[]{:S(2)}, u32[]{:S(2)}) collective-permute-start(f32[4,8,1024]{2,1,0:T(8,128)S(1)} %get-tuple-element.42), channel_id=1, source_target_pairs={{0,56},{8,48},{16,40},{24,32},{32,24},{40,16},{48,8},{56,0},{64,12... | collective-permute-start | bytes 393224 | tf_op jit(solution)/shard_map/ppermute | solution.py:352
  41.0 7.4 %collective-permute-start.11 = (f32[8,1024]{1,0:T(8,128)S(1)}, f32[8,1024]{1,0:T(8,128)S(1)}, u32[]{:S(2)}, u32[]{:S(2)}) collective-permute-start(f32[8,1024]{1,0:T(8,128)S(1)} %get-tuple-element.45), channel_id=1, source_target_pairs={{0,64},{8,72},{16,80},{24,88},{32,96},{40,104},{48,112},{56,120},{... | collective-permute-start | bytes 98312 | tf_op jit(solution)/shard_map/ppermute | solution.py:352
  42.7 7.9 %collective-permute-start.12 = (f32[8,1024]{1,0:T(8,128)S(1)}, f32[8,1024]{1,0:T(8,128)S(1)}, u32[]{:S(2)}, u32[]{:S(2)}) collective-permute-start(f32[8,1024]{1,0:T(8,128)S(1)} %get-tuple-element.46), channel_id=1, source_target_pairs={{0,128},{8,136},{16,144},{24,152},{32,160},{40,168},{48,176},{56,1... | collective-permute-start | bytes 98312 | tf_op jit(solution)/shard_map/ppermute | solution.py:352
  48.4 6.0 %collective-permute-start.13 = (f32[8,1024]{1,0:T(8,128)S(1)}, f32[8,1024]{1,0:T(8,128)S(1)}, u32[]{:S(2)}, u32[]{:S(2)}) collective-permute-start(f32[8,1024]{1,0:T(8,128)S(1)} %get-tuple-element.47), channel_id=1, source_target_pairs={{0,192},{8,200},{16,208},{24,216},{32,224},{40,232},{48,240},{56,2... | collective-permute-start | bytes 98312 | tf_op jit(solution)/shard_map/ppermute | solution.py:352

commit v2 on v1

v2 whole, which is shorter than its diff:
```python
import math

import jax
import jax.numpy as jnp
from jax import lax
from jax.experimental import pallas as pl
from jax.experimental.pallas import tpu as pltpu
from jax.sharding import PartitionSpec as P

LIGHT_X = 0.48
LIGHT_Y = 0.6
LIGHT_Z = 0.64
UNIT = 2048.0
LANES = 128
MIB = 1024 * 1024
F32 = jnp.float32
ORDER8 = (1, 7, 6, 5, 4, 3, 2, 0)
ORDER4 = (1, 2, 3, 0)


def params(mib):
    return pltpu.CompilerParams(vmem_limit_bytes=mib * MIB)


def faces_kernel(d_ref, t_ref, za_ref, zb_ref, ya_ref, yb_ref, table_ref, low, high, t, sems):
    depth, rows = d_ref.shape[0], d_ref.shape[1]
    slab_odd = lax.axis_index("slab") & 1
    lat_odd = lax.axis_index("lat") & 1
    last = depth - 1
    copies = [
        pltpu.make_async_copy(d_ref.at[last - last * slab_odd], za_ref, sems.at[0]),
        pltpu.make_async_copy(d_ref.at[last * slab_odd], zb_ref, sems.at[1]),
        pltpu.make_async_copy(d_ref.at[:, pl.ds(0, 8)], low, sems.at[2]),
        pltpu.make_async_copy(d_ref.at[:, pl.ds(rows - 8, 8)], high, sems.at[3]),
        pltpu.make_async_copy(t_ref, t, sems.at[4]),
    ]
    for copy in copies:
        copy.start()
    copies[4].wait()
    units = (t[...].astype(F32) * UNIT).astype(jnp.int32)
    for pair in range(2):
        word = units[2 * pair : 2 * pair + 1] | (units[2 * pair + 1 : 2 * pair + 2] << 16)
        for half in range(2):
            table_ref[2 * pair + half] = jnp.broadcast_to(
                word[:, half * LANES : (half + 1) * LANES], (8, LANES)
            )
    copies[2].wait()
    copies[3].wait()
    odd = lat_odd == 1
    for k in range(depth):
        first, final = low[k, 0:1], high[k, 7:8]
        ya_ref[k : k + 1, :] = jnp.where(odd, first, final)
        yb_ref[k : k + 1, :] = jnp.where(odd, final, first)
    copies[0].wait()
    copies[1].wait()


def faces(density, transfer):
    depth, rows, line = density.shape
    return pl.pallas_call(
        faces_kernel,
        out_shape=[
            jax.ShapeDtypeStruct((rows, line), F32),
            jax.ShapeDtypeStruct((rows, line), F32),
            jax.ShapeDtypeStruct((depth, line), F32),
            jax.ShapeDtypeStruct((depth, line), F32),
            jax.ShapeDtypeStruct((4, 8, LANES), jnp.int32),
        ],
        in_specs=[pl.BlockSpec(memory_space=pl.ANY)] * 2,
        out_specs=[pl.BlockSpec(memory_space=pl.ANY)] * 2
        + [pl.BlockSpec(memory_space=pltpu.VMEM)] * 3,
        scratch_shapes=[
            pltpu.VMEM((depth, 8, line), F32),
            pltpu.VMEM((depth, 8, line), F32),
            pltpu.VMEM(transfer.shape, transfer.dtype),
            pltpu.SemaphoreType.DMA((5,)),
        ],
        compiler_params=params(4),
        name="faces",
    )(density, transfer)


def columns_of(table, column):
    numbers = lax.GatherDimensionNumbers(
        offset_dims=(),
        collapsed_slice_dims=(1,),
        start_index_map=(1,),
        operand_batching_dims=(0,),
        start_indices_batching_dims=(0,),
    )
    return lax.gather(
        table, column[..., None], numbers, (1, 1), mode=lax.GatherScatterMode.PROMISE_IN_BOUNDS
    )


def look_up(table, bins):
    column = bins & (LANES - 1)
    upper = bins >= LANES
    values = []
    for low_half, high_half in table:
        word = jnp.where(upper, columns_of(high_half, column), columns_of(low_half, column))
        values += [(word & 0xFFFF).astype(F32), (word >> 16).astype(F32)]
    return values


def look_kernel(spacing, d_hbm, b_hbm, o_hbm, t_ref, d_ref, w_ref, l_ref, o_ref, b, sems):
    depth, rows, line = d_hbm.shape

    def copies(t):
        at = pl.ds(pl.multiple_of(t * 8, 8), 8)
        inner = pl.ds(pl.multiple_of(t * 8 + 8, 8), 8)
        return [
            pltpu.make_async_copy(b_hbm.at[:, at], b.at[:, at], sems.at[0, t]),
            pltpu.make_async_copy(d_hbm.at[:, at], d_ref.at[:, inner], sems.at[1, t]),
            pltpu.make_async_copy(o_hbm.at[at], o_ref.at[at], sems.at[2, t]),
        ]

    for t in range(rows // 8):
        for copy in copies(t):
            copy.start()
    table = [[t_ref[2 * pair + half] for half in range(2)] for pair in range(2)]
    scale = -spacing / (UNIT * math.log(2.0))

    def tile(t, carry):
        at = pl.ds(pl.multiple_of(t * 8, 8), 8)
        inner = pl.ds(pl.multiple_of(t * 8 + 8, 8), 8)
        for copy in copies(t):
            copy.wait()
        for c in range(line // LANES):
            cols = slice(c * LANES, (c + 1) * LANES)
            reverse = o_ref[at, cols] == 1
            passed, colors = [], []
            for k in range(depth):
                *color, extinction = look_up(table, b[k, at, cols])
                passed.append(jnp.exp2(extinction * scale * d_ref[k, inner, cols]))
                colors.append(color)
            t0, t1, t2, t3 = passed
            front, back = t0 * t1, t2 * t3
            ahead = [
                jnp.where(reverse, t1 * back, 1.0),
                jnp.where(reverse, back, t0),
                jnp.where(reverse, t3, front),
                jnp.where(reverse, 1.0, front * t2),
            ]
            for k in range(depth):
                weight = (1.0 - passed[k]) * (1.0 / UNIT) * ahead[k]
                for i in range(3):
                    w_ref[k, i, at, cols] = colors[k][i] * weight
            l_ref[at, cols] = front * back
        return carry

    lax.fori_loop(0, rows // 8, tile, 0)


def look(density, bins, order, table, spacing):
    depth, rows, line = density.shape
    vmem = pl.BlockSpec(memory_space=pltpu.VMEM)
    hbm = pl.BlockSpec(memory_space=pl.ANY)
    cells = depth * rows * line
    return pl.pallas_call(
        lambda *refs: look_kernel(spacing, *refs),
        out_shape=[
            jax.ShapeDtypeStruct((depth, rows + 16, line), F32),
            jax.ShapeDtypeStruct((depth, 3, rows, line), F32),
            jax.ShapeDtypeStruct((rows, line), F32),
            jax.ShapeDtypeStruct((rows, line), jnp.int32),
        ],
        in_specs=[hbm] * 3 + [vmem],
        out_specs=[vmem] * 4,
        scratch_shapes=[
            pltpu.VMEM((depth, rows, line), jnp.int32),
            pltpu.SemaphoreType.DMA((3, rows // 8)),
        ],
        compiler_params=params(12),
        cost_estimate=pl.CostEstimate(
            flops=50 * cells, bytes_accessed=12 * cells, transcendentals=cells
        ),
        name="look",
    )(density, bins, order, table)


def slopes_kernel(d_in, w_ref, ya_ref, yb_ref, d, c_ref, a_ref, n_ref):
    depth, rows, line = d.shape[0], d.shape[1] - 16, d.shape[2]
    chunks = line // LANES
    lat = lax.axis_index("lat")
    lat_odd = (lat & 1) == 1
    keep_low = jnp.where(lat == 0, 0.0, 1.0).astype(F32)
    keep_high = jnp.where(lat == lax.axis_size("lat") - 1, 0.0, 1.0).astype(F32)
    for k in range(depth):
        from_a, from_b = ya_ref[k : k + 1, :], yb_ref[k : k + 1, :]
        d[k, 7:8, :] = jnp.where(lat_odd, from_a, from_b) * keep_low
        d[k, rows + 8 : rows + 9, :] = jnp.where(lat_odd, from_b, from_a) * keep_high
    lane = lax.broadcasted_iota(jnp.int32, (8, LANES), 1)
    sub = lax.broadcasted_iota(jnp.int32, (8, LANES), 0)
    first_lane, last_lane = lane == 0, lane == LANES - 1
    first_sub, last_sub = sub == 0, sub == 7

    def tile(t, carry):
        base = pl.multiple_of(t * 8, 8)
        at = pl.ds(base, 8)
        for c in range(chunks):
            cols = slice(c * LANES, (c + 1) * LANES)

            def cell(k, row, column=c):
                return d[k, pl.ds(row, 8), column * LANES : (column + 1) * LANES]

            total = [None, None, None]
            for k in range(depth):
                here = cell(k, base + 8)
                before, after = cell(k, base), cell(k, base + 16)
                left = cell(k, base + 8, c - 1) if c > 0 else jnp.zeros_like(here)
                right = cell(k, base + 8, c + 1) if c < chunks - 1 else jnp.zeros_like(here)
                step_x = pltpu.roll(jnp.where(first_lane, right, here), LANES - 1, 1) - pltpu.roll(
                    jnp.where(last_lane, left, here), 1, 1
                )
                step_y = pltpu.roll(jnp.where(first_sub, after, here), 7, 0) - pltpu.roll(
                    jnp.where(last_sub, before, here), 1, 0
                )
                tilt = LIGHT_X * step_x + LIGHT_Y * step_y
                norm = step_x * step_x + step_y * step_y + 1.0
                if k in (0, depth - 1):
                    a_ref[min(k, 1), at, cols] = tilt
                    n_ref[min(k, 1), at, cols] = norm
                    continue
                step_z = cell(k + 1, base + 8) - cell(k - 1, base + 8)
                shade = 1.0 + (tilt + LIGHT_Z * step_z) * lax.rsqrt(norm + step_z * step_z)
                for i in range(3):
                    term = w_ref[k, i, at, cols] * shade
                    total[i] = term if total[i] is None else total[i] + term
            for i in range(3):
                c_ref[i, at, cols] = total[i]
        return carry

    lax.fori_loop(0, rows // 8, tile, 0)


def slopes(density, weight, ya, yb):
    depth, rows, line = density.shape
    rows -= 16
    vmem = pl.BlockSpec(memory_space=pltpu.VMEM)
    cells = depth * rows * line
    return pl.pallas_call(
        slopes_kernel,
        out_shape=[
            jax.ShapeDtypeStruct(density.shape, F32),
            jax.ShapeDtypeStruct((3, rows, line), F32),
            jax.ShapeDtypeStruct((2, rows, line), F32),
            jax.ShapeDtypeStruct((2, rows, line), F32),
        ],
        in_specs=[vmem] * 4,
        out_specs=[vmem] * 4,
        input_output_aliases={0: 0},
        compiler_params=params(12),
        cost_estimate=pl.CostEstimate(
            flops=50 * cells, bytes_accessed=12 * cells, transcendentals=cells
        ),
        name="slopes",
    )(density, weight, ya, yb)


def swap_pieces(tiles, sub):
    for size in (4, 2):
        keep = (sub & size) == 0
        step = size // 2
        result = list(tiles)
        for i in range(4):
            if i & step == 0:
                a, b = tiles[i], tiles[i | step]
                result[i] = jnp.where(keep, a, pltpu.roll(b, size, 0))
                result[i | step] = jnp.where(keep, pltpu.roll(a, 8 - size, 0), b)
        tiles = result
    return tiles


def edges_kernel(d_ref, za_ref, zb_ref, o_ref, c_ref, w_ref, l_ref, a_ref, n_ref, *rest):
    outs, mask_ref, s = rest[:8], rest[8], rest[9]
    depth, line = d_ref.shape[0], d_ref.shape[2]
    slab = lax.axis_index("slab")
    slab_odd = (slab & 1) == 1
    keep_low = jnp.where(slab == 0, 0.0, 1.0).astype(F32)
    keep_high = jnp.where(slab == lax.axis_size("slab") - 1, 0.0, 1.0).astype(F32)
    sub = lax.broadcasted_iota(jnp.int32, (8, LANES), 0)
    chunks = line // LANES

    def part(index, carry):
        half, c = index // chunks, index % chunks
        cols = pl.ds(pl.multiple_of(c * LANES, LANES), LANES)
        channels = [[] for _ in range(5)]
        for quarter in range(4):
            at = pl.ds(pl.multiple_of(16 * quarter + 8 * half, 8), 8)
            inner = pl.ds(pl.multiple_of(16 * quarter + 8 * half + 8, 8), 8)
            from_a, from_b = za_ref[at, cols], zb_ref[at, cols]
            below = jnp.where(slab_odd, from_a, from_b) * keep_low
            above = jnp.where(slab_odd, from_b, from_a) * keep_high
            total = [c_ref[i, at, cols] for i in range(3)]
            steps = (d_ref[1, inner, cols] - below, above - d_ref[depth - 2, inner, cols])
            for edge in range(2):
                step_z = steps[edge]
                shade = 1.0 + (a_ref[edge, at, cols] + LIGHT_Z * step_z) * lax.rsqrt(
                    n_ref[edge, at, cols] + step_z * step_z
                )
                for i in range(3):
                    total[i] = total[i] + w_ref[edge * (depth - 1), i, at, cols] * shade
            for i in range(3):
                channels[i].append(total[i])
            channels[3].append(l_ref[at, cols])
            channels[4].append(o_ref[at, cols].astype(F32))
        for i in range(5):
            for piece, value in enumerate(swap_pieces(channels[i], sub)):
                s[4 * half + piece, i, :, cols] = value
        return carry

    lax.fori_loop(0, 2 * chunks, part, 0)
    place = slab & 7
    for j in range(8):
        for i in range(4):
            outs[j][i] = s[place ^ j, i]
    mask_ref[...] = s[place, 4]


def edges(density, za, zb, order, color, weight, light, tilt, norm):
    depth, rows, line = density.shape
    rows -= 16
    vmem = pl.BlockSpec(memory_space=pltpu.VMEM)
    return pl.pallas_call(
        edges_kernel,
        out_shape=[jax.ShapeDtypeStruct((4, 8, line), F32)] * 8
        + [jax.ShapeDtypeStruct((8, line), F32)],
        in_specs=[vmem] * 9,
        out_specs=[vmem] * 9,
        scratch_shapes=[pltpu.VMEM((8, 5, 8, line), F32)],
        compiler_params=params(12),
        cost_estimate=pl.CostEstimate(
            flops=40 * depth * rows * line, bytes_accessed=4 * depth * rows * line, transcendentals=depth * rows * line
        ),
        name="edges",
    )(density, za, zb, order, color, weight, light, tilt, norm)


def merge(a, b, b_first):
    front = [jnp.where(b_first, y, x) for x, y in zip(a, b)]
    back = [jnp.where(b_first, x, y) for x, y in zip(a, b)]
    return [front[i] + front[3] * back[i] for i in range(3)] + [front[3] * back[3]]


def merge_tree(blocks, mask, place):
    bit = 0
    while len(blocks) > 1:
        b_first = jnp.logical_xor(mask > 0.5, (place >> bit & 1) == 1)
        blocks = [merge(blocks[i], blocks[i + 1], b_first) for i in range(0, len(blocks), 2)]
        bit += 1
    return blocks[0]


def eight_kernel(*refs):
    ins, mask_ref, outs, own_mask = refs[:8], refs[8], refs[9:13], refs[13]
    line = mask_ref.shape[1]
    slab = lax.axis_index("slab")
    place, quarter = slab & 7, slab >> 3
    sub = lax.broadcasted_iota(jnp.int32, (8, LANES), 0) // 2

    def part(c, carry):
        cols = pl.ds(pl.multiple_of(c * LANES, LANES), LANES)
        mask = mask_ref[:, cols]
        blocks = [[ins[ORDER8.index(j)][i, :, cols] for i in range(4)] for j in range(8)]
        merged = merge_tree(blocks, mask, place)
        for j in range(4):
            target = quarter ^ j
            packed = None
            for i in range(4):
                moved = pltpu.roll(merged[i], (2 * i + 8 - 2 * target) & 7, 0)
                packed = moved if packed is None else jnp.where(sub == i, moved, packed)
            outs[j][:, cols] = packed
        own_mask[:, cols] = pltpu.roll(mask, (8 - 2 * quarter) & 7, 0)
        return carry

    lax.fori_loop(0, line // LANES, part, 0)


def merge_eight(blocks, mask):
    line = mask.shape[1]
    vmem = pl.BlockSpec(memory_space=pltpu.VMEM)
    return pl.pallas_call(
        eight_kernel,
        out_shape=[jax.ShapeDtypeStruct((8, line), F32)] * 5,
        in_specs=[vmem] * 9,
        out_specs=[vmem] * 5,
        compiler_params=params(6),
        name="merge_eight",
    )(*[blocks[j] for j in ORDER8], mask)


def four_kernel(*refs):
    ins, mask_ref, out = refs[:4], refs[4], refs[5]
    place = lax.axis_index("slab") >> 3
    mask = mask_ref[0:2, :]
    blocks = [[ins[ORDER4.index(j)][2 * i : 2 * i + 2, :] for i in range(4)] for j in range(4)]
    merged = merge_tree(blocks, mask, place)
    for i in range(3):
        out[i] = merged[i]
    out[3] = 1.0 - merged[3]


def merge_four(blocks, mask):
    line = mask.shape[1]
    vmem = pl.BlockSpec(memory_space=pltpu.VMEM)
    return pl.pallas_call(
        four_kernel,
        out_shape=jax.ShapeDtypeStruct((4, 2, line), F32),
        in_specs=[vmem] * 5,
        out_specs=vmem,
        compiler_params=params(4),
        name="merge_four",
    )(*[blocks[j] for j in ORDER4], mask)


def swap(block, axis, step):
    count = lax.axis_size(axis)
    return lax.ppermute(block, axis, [(i, i ^ step) for i in range(count)])


def swap_odd(block, axis):
    count = lax.axis_size(axis)
    route = []
    for i in range(1, count, 2):
        route += [(i, (i + 1) % count), ((i + 1) % count, i)]
    return lax.ppermute(block, axis, route)


def shards(density, bins, transfer, depth_order):
    depth_cells = density.shape[0]
    spacing = 1.5 / (depth_cells * lax.axis_size("slab"))
    density, bins, transfer, depth_order = (
        pltpu.with_memory_space_constraint(x, pltpu.HBM)
        for x in (density, bins, transfer, depth_order)
    )
    za, zb, ya, yb, table = faces(density, transfer)
    za, zb = swap(za, "slab", 1), swap_odd(zb, "slab")
    ya, yb = swap(ya, "lat", 1), swap_odd(yb, "lat")
    density, weight, light, order = look(density, bins, depth_order, table, spacing)
    density, color, tilt, norm = slopes(density, weight, ya, yb)
    *blocks, mask = edges(density, za, zb, order, color, weight, light, tilt, norm)
    blocks = blocks[:1] + [swap(blocks[j], "slab", j) for j in range(1, 8)]
    *quarters, mask = merge_eight(blocks, mask)
    quarters = quarters[:1] + [swap(quarters[j], "slab", 8 * j) for j in range(1, 4)]
    return merge_four(quarters, mask)


def solution(mesh):
    return jax.shard_map(
        shards,
        mesh=mesh,
        in_specs=(P("slab", "lat", None), P("slab", "lat", None), P(), P("lat", None)),
        out_specs=P(None, ("lat", "slab"), None),
        check_vma=False,
    )
```

time: 55.3 us -> 46.3 us (0.84)
  waiting for transfers between devices: 17.1 us -> 11.7 us
  local copies, waits for them, and re-layouts: 4.02 us -> 0 us
  Pallas kernels: 7.06 us -> 8.09 us
    unnamed x12 -> x0, local copies, waits for them, and re-layouts: 4.02 us -> none
    ppermute x12, waiting for transfers between devices: 15.2 us -> 11.4 us  [swap(): return lax.ppermute(block, axis, [(i, i ^ step) for i in range(count)])]
    ppermute x2, waiting for transfers between devices: 1.99 us -> 0.33 us  [swap_odd(): return lax.ppermute(block, axis, route)]
    pallas_call x1 -> x2, Pallas kernels: 3.56 us -> 4.99 us  [the longest x1 3.84 us: look(): pl.pallas_call(lambda *refs: look_kernel(spacing, *refs), out_shape=[jax....]
    pallas_call x1, Pallas kernels: 2.38 us -> 0.99 us  [edges(): pl.pallas_call(edges_kernel, out_shape=[jax.ShapeDtypeStruct((4, 8, line)...]
    pallas_call x1, Pallas kernels: 0.16 us -> 1.15 us  [faces(): pl.pallas_call(faces_kernel, out_shape=[jax.ShapeDtypeStruct((rows, line)...]
    ppermute x12, starting transfers between devices: 18.7 us -> 18.2 us  [swap(): return lax.ppermute(block, axis, [(i, i ^ step) for i in range(count)])]
  transfers between devices with their start and end apart: 14 -> 14, of which waited for: 9 -> 6; matrix products, arithmetic and copies ran while one was open for 0% -> 0% of each run, Pallas kernels for 6% -> 11%
where the time goes in v2:
time: 46.3 us; the launch traced here: 46.2 us
  starting transfers between devices  26.3 us (57%)
  waiting for transfers between devices  11.7 us (25%)
  Pallas kernels  8.09 us (17%)
    ppermute x12, starting transfers between devices, swap(): return lax.ppermute(block, axis, [(i, i ^ step) for i in range(count)])  18.2 us
    ppermute x12, waiting for transfers between devices, swap(): return lax.ppermute(block, axis, [(i, i ^ step) for i in range(count)])  11.4 us
    ppermute x2, starting transfers between devices, swap_odd(): return lax.ppermute(block, axis, route)  8.12 us
    pallas_call x1, Pallas kernels, look(): pl.pallas_call(lambda *refs: look_kernel(spacing, *refs), out_shape=[jax....  3.84 us
    pallas_call x1, Pallas kernels, faces(): pl.pallas_call(faces_kernel, out_shape=[jax.ShapeDtypeStruct((rows, line)...  1.15 us
    pallas_call x1, Pallas kernels, slopes(): pl.pallas_call(slopes_kernel, out_shape=[jax.ShapeDtypeStruct(density.sha...  1.15 us
    pallas_call x1, Pallas kernels, edges(): pl.pallas_call(edges_kernel, out_shape=[jax.ShapeDtypeStruct((4, 8, line)...  0.99 us
  transfers between devices with their start and end apart: 14, of which 6 were waited for; matrix products, arithmetic and copies ran while one was open for 0% of the time, Pallas kernels for 11%

profile of v2, /device:TPU:2, one launch (start us, length us, event | category | flops | bytes accessed | tf_op | source)
XLA Modules:
  0.0 46.2 jit_solution(18167546453173027075)
XLA Ops:
  0.0 1.2 %faces.1 = (f32[64,1024]{1,0:T(8,128)S(1)}, f32[64,1024]{1,0:T(8,128)S(1)}, f32[4,1024]{1,0:T(4,128)S(1)}, f32[4,1024]{1,0:T(4,128)S(1)}, s32[4,8,128]{2,1,0:T(8,128)S(1)}) custom-call(f32[4,64,1024]{2,1,0:T(8,128)} %refs_0_.1, bf16[4,256]{1,0:T(4,128)(2,1)} %t_ref.1), custom_call_target="tpu_custom_call" | custom-call | tf_op jit(solution)/shard_map/faces/pallas_call | solution.py:60
  1.2 1.7 %collective-permute-start.2 = (f32[64,1024]{1,0:T(8,128)S(1)}, f32[64,1024]{1,0:T(8,128)S(1)}, u32[]{:S(2)}, u32[]{:S(2)}) collective-permute-start(f32[64,1024]{1,0:T(8,128)S(1)} %get-tuple-element.38), channel_id=1, source_target_pairs={{0,8},{8,0},{16,24},{24,16},{32,40},{40,32},{48,56},{56,48},{64,72... | collective-permute-start | bytes 786440 | tf_op jit(solution)/shard_map/ppermute | solution.py:419
  2.8 7.5 %collective-permute-start.3 = (f32[64,1024]{1,0:T(8,128)S(1)}, f32[64,1024]{1,0:T(8,128)S(1)}, u32[]{:S(2)}, u32[]{:S(2)}) collective-permute-start(f32[64,1024]{1,0:T(8,128)S(1)} %get-tuple-element.39), channel_id=1, source_target_pairs={{8,16},{16,8},{24,32},{32,24},{40,48},{48,40},{56,64},{64,56},{72,... | collective-permute-start | bytes 786440 | tf_op jit(solution)/shard_map/ppermute | solution.py:427
  10.3 0.0 collective-permute-start
  10.3 0.6 %collective-permute-start.1 = (f32[4,1024]{1,0:T(4,128)S(1)}, f32[4,1024]{1,0:T(4,128)S(1)}, u32[]{:S(2)}, u32[]{:S(2)}) collective-permute-start(f32[4,1024]{1,0:T(4,128)S(1)} %get-tuple-element.36), channel_id=1, source_target_pairs={{1,2},{2,1},{3,4},{4,3},{5,6},{6,5},{7,0},{0,7},{9,10},{10,9},{11,... | collective-permute-start | bytes 49160 | tf_op jit(solution)/shard_map/ppermute | solution.py:427
  11.0 3.8 %look.1 = (f32[4,80,1024]{2,1,0:T(8,128)S(1)}, f32[4,3,64,1024]{3,2,1,0:T(8,128)S(1)}, f32[64,1024]{1,0:T(8,128)S(1)}, s32[64,1024]{1,0:T(8,128)S(1)}) custom-call(f32[4,64,1024]{2,1,0:T(8,128)} %refs_0_.1, s32[4,64,1024]{2,1,0:T(8,128)} %refs_1_.1, s32[64,1024]{1,0:T(8,128)} %refs_2_.1, s32[4,8,128]{2,1,0:T(8,128)S(1)} %get-tuple-element.32.refs_3_), custom_call_target="tpu_custom_call" | custom-call | flops 13107200 | bytes 3145728 | tf_op jit(solution)/shard_map/look/pallas_call | solution.py:160
  14.8 0.0 collective-permute-done.ya_ref
  14.8 0.0 collective-permute-done.1.yb_ref
  14.8 1.2 %slopes.1 = (f32[4,80,1024]{2,1,0:T(8,128)S(1)}, f32[3,64,1024]{2,1,0:T(8,128)S(1)}, f32[2,64,1024]{2,1,0:T(8,128)S(1)}, f32[2,64,1024]{2,1,0:T(8,128)S(1)}) custom-call(f32[4,80,1024]{2,1,0:T(8,128)S(1)} %get-tuple-element.33.d_in, f32[4,3,64,1024]{3,2,1,0:T(8,128)S(1)} %get-tuple-element.34.w_ref, ...), custom_call_target="tpu_custom_call", output_to_operand_aliasing={{0}: (0, {})} | custom-call | flops 13107200 | bytes 3145728 | tf_op jit(solution)/shard_map/slopes/pallas_call | solution.py:242
  16.0 0.0 collective-permute-done.2.za_ref
  16.0 0.3 collective-permute-done.3.zb_ref
  16.3 1.0 %edges.1 = (f32[4,8,1024]{2,1,0:T(8,128)S(1)}, f32[4,8,1024]{2,1,0:T(8,128)S(1)}, f32[4,8,1024]{2,1,0:T(8,128)S(1)}, f32[4,8,1024]{2,1,0:T(8,128)S(1)}, f32[4,8,...) custom-call(f32[4,80,1024]{2,1,0:T(8,128)S(1)} %get-tuple-element.37, ...), custom_call_target="tpu_custom_call" | custom-call | flops 10485760 | bytes 1048576 | tf_op jit(solution)/shard_map/edges/pallas_call | solution.py:325
  17.3 0.1 collective-permute-start.4
  17.4 0.1 collective-permute-start.5
  17.5 4.9 %collective-permute-start.6 = (f32[4,8,1024]{2,1,0:T(8,128)S(1)}, f32[4,8,1024]{2,1,0:T(8,128)S(1)}, u32[]{:S(2)}, u32[]{:S(2)}) collective-permute-start(f32[4,8,1024]{2,1,0:T(8,128)S(1)} %get-tuple-element.47), channel_id=1, source_target_pairs={{0,48},{8,56},{16,32},{24,40},{32,16},{40,24},{48,0},{56,8},{64,11... | collective-permute-start | bytes 393224 | tf_op jit(solution)/shard_map/ppermute | solution.py:419
  22.4 0.0 collective-permute-start.7
  22.4 1.6 %collective-permute-start.8 = (f32[4,8,1024]{2,1,0:T(8,128)S(1)}, f32[4,8,1024]{2,1,0:T(8,128)S(1)}, u32[]{:S(2)}, u32[]{:S(2)}) collective-permute-start(f32[4,8,1024]{2,1,0:T(8,128)S(1)} %get-tuple-element.49), channel_id=1, source_target_pairs={{0,32},{8,40},{16,48},{24,56},{32,0},{40,8},{48,16},{56,24},{64,96... | collective-permute-start | bytes 393224 | tf_op jit(solution)/shard_map/ppermute | solution.py:419
  24.0 3.6 %collective-permute-done.4.refs_0_ = f32[4,8,1024]{2,1,0:T(8,128)S(1)} collective-permute-done((f32[4,8,1024]{2,1,0:T(8,128)S(1)}, f32[4,8,1024]{2,1,0:T(8,128)S(1)}, u32[]{:S(2)}, u32[]{:S(2)}) %collective-permute-start.4) | collective-permute-done | bytes 131104 | tf_op jit(solution)/shard_map/ppermute | solution.py:419
  27.6 0.0 collective-permute-start.9
  27.6 0.0 collective-permute-done.5.refs_1_
  27.6 3.3 %collective-permute-start.10 = (f32[4,8,1024]{2,1,0:T(8,128)S(1)}, f32[4,8,1024]{2,1,0:T(8,128)S(1)}, u32[]{:S(2)}, u32[]{:S(2)}) collective-permute-start(f32[4,8,1024]{2,1,0:T(8,128)S(1)} %get-tuple-element.51), channel_id=1, source_target_pairs={{0,16},{8,24},{16,0},{24,8},{32,48},{40,56},{48,32},{56,40},{64,80... | collective-permute-start | bytes 393224 | tf_op jit(solution)/shard_map/ppermute | solution.py:419
  30.9 0.0 collective-permute-done.6.refs_2_
  30.9 0.0 collective-permute-done.7.refs_3_
  30.9 0.2 collective-permute-done.8.refs_4_
  31.0 5.1 %collective-permute-done.9.refs_5_ = f32[4,8,1024]{2,1,0:T(8,128)S(1)} collective-permute-done((f32[4,8,1024]{2,1,0:T(8,128)S(1)}, f32[4,8,1024]{2,1,0:T(8,128)S(1)}, u32[]{:S(2)}, u32[]{:S(2)}) %collective-permute-start.9) | collective-permute-done | bytes 131104 | tf_op jit(solution)/shard_map/ppermute | solution.py:419
  36.1 0.0 collective-permute-done.10.refs_6_
  36.1 0.3 merge_eight.1
  36.4 0.1 collective-permute-start.11
  36.5 3.0 %collective-permute-start.12 = (f32[8,1024]{1,0:T(8,128)S(1)}, f32[8,1024]{1,0:T(8,128)S(1)}, u32[]{:S(2)}, u32[]{:S(2)}) collective-permute-start(f32[8,1024]{1,0:T(8,128)S(1)} %get-tuple-element.55), channel_id=1, source_target_pairs={{0,128},{8,136},{16,144},{24,152},{32,160},{40,168},{48,176},{56,1... | collective-permute-start | bytes 98312 | tf_op jit(solution)/shard_map/ppermute | solution.py:419
  39.5 3.5 %collective-permute-start.13 = (f32[8,1024]{1,0:T(8,128)S(1)}, f32[8,1024]{1,0:T(8,128)S(1)}, u32[]{:S(2)}, u32[]{:S(2)}) collective-permute-start(f32[8,1024]{1,0:T(8,128)S(1)} %get-tuple-element.56), channel_id=1, source_target_pairs={{0,192},{8,200},{16,208},{24,216},{32,224},{40,232},{48,240},{56,2... | collective-permute-start | bytes 98312 | tf_op jit(solution)/shard_map/ppermute | solution.py:419
  43.0 0.0 collective-permute-done.11.refs_0_
  43.0 1.4 %collective-permute-done.12.refs_1_ = f32[8,1024]{1,0:T(8,128)S(1)} collective-permute-done((f32[8,1024]{1,0:T(8,128)S(1)}, f32[8,1024]{1,0:T(8,128)S(1)}, u32[]{:S(2)}, u32[]{:S(2)}) %collective-permute-start.12) | collective-permute-done | bytes 32800 | tf_op jit(solution)/shard_map/ppermute | solution.py:419
  44.4 1.1 %collective-permute-done.13.refs_2_ = f32[8,1024]{1,0:T(8,128)S(1)} collective-permute-done((f32[8,1024]{1,0:T(8,128)S(1)}, f32[8,1024]{1,0:T(8,128)S(1)}, u32[]{:S(2)}, u32[]{:S(2)}) %collective-permute-start.13) | collective-permute-done | bytes 32800 | tf_op jit(solution)/shard_map/ppermute | solution.py:419
  45.5 0.7 %merge_four.1 = f32[4,2,1024]{2,1,0:T(2,128)} custom-call(f32[8,1024]{1,0:T(8,128)S(1)} %collective-permute-done.11.refs_0_, f32[8,1024]{1,0:T(8,128)S(1)} %collective-permute-done.12.refs_1_, f32[8,1024]{1,0:T(8,128)S(1)} %collective-permute-done.13.refs_2_, f32[8,1024]{1,0:T(8,128)S(1)} %get-tuple-element.57.refs_3_, f32[8,1024]{1,0:T(8,128)S(1)} %get-tuple-element.58.refs_4_), custom_call_target="tpu_custom_call" | custom-call | tf_op jit(solution)/shard_map/merge_four/pallas_call | solution.py:407
Async XLA Ops:
  1.2 14.8 %collective-permute-start.2 = (f32[64,1024]{1,0:T(8,128)S(1)}, f32[64,1024]{1,0:T(8,128)S(1)}, u32[]{:S(2)}, u32[]{:S(2)}) collective-permute-start(f32[64,1024]{1,0:T(8,128)S(1)} %get-tuple-element.38), channel_id=1, source_target_pairs={{0,8},{8,0},{16,24},{24,16},{32,40},{40,32},{48,56},{56,48},{64,72... | collective-permute-start | bytes 786440 | tf_op jit(solution)/shard_map/ppermute | solution.py:419
  2.8 13.5 %collective-permute-start.3 = (f32[64,1024]{1,0:T(8,128)S(1)}, f32[64,1024]{1,0:T(8,128)S(1)}, u32[]{:S(2)}, u32[]{:S(2)}) collective-permute-start(f32[64,1024]{1,0:T(8,128)S(1)} %get-tuple-element.39), channel_id=1, source_target_pairs={{8,16},{16,8},{24,32},{32,24},{40,48},{48,40},{56,64},{64,56},{72,... | collective-permute-start | bytes 786440 | tf_op jit(solution)/shard_map/ppermute | solution.py:427
  10.3 4.5 %collective-permute-start = (f32[4,1024]{1,0:T(4,128)S(1)}, f32[4,1024]{1,0:T(4,128)S(1)}, u32[]{:S(2)}, u32[]{:S(2)}) collective-permute-start(f32[4,1024]{1,0:T(4,128)S(1)} %get-tuple-element.35), channel_id=1, source_target_pairs={{0,1},{1,0},{2,3},{3,2},{4,5},{5,4},{6,7},{7,6},{8,9},{9,8},{10,11... | collective-permute-start | bytes 49160 | tf_op jit(solution)/shard_map/ppermute | solution.py:419
  10.3 4.5 %collective-permute-start.1 = (f32[4,1024]{1,0:T(4,128)S(1)}, f32[4,1024]{1,0:T(4,128)S(1)}, u32[]{:S(2)}, u32[]{:S(2)}) collective-permute-start(f32[4,1024]{1,0:T(4,128)S(1)} %get-tuple-element.36), channel_id=1, source_target_pairs={{1,2},{2,1},{3,4},{4,3},{5,6},{6,5},{7,0},{0,7},{9,10},{10,9},{11,... | collective-permute-start | bytes 49160 | tf_op jit(solution)/shard_map/ppermute | solution.py:427
  17.3 10.3 %collective-permute-start.4 = (f32[4,8,1024]{2,1,0:T(8,128)S(1)}, f32[4,8,1024]{2,1,0:T(8,128)S(1)}, u32[]{:S(2)}, u32[]{:S(2)}) collective-permute-start(f32[4,8,1024]{2,1,0:T(8,128)S(1)} %get-tuple-element.45), channel_id=1, source_target_pairs={{0,8},{8,0},{16,24},{24,16},{32,40},{40,32},{48,56},{56,48},{64,72... | collective-permute-start | bytes 393224 | tf_op jit(solution)/shard_map/ppermute | solution.py:419
  17.4 10.2 %collective-permute-start.5 = (f32[4,8,1024]{2,1,0:T(8,128)S(1)}, f32[4,8,1024]{2,1,0:T(8,128)S(1)}, u32[]{:S(2)}, u32[]{:S(2)}) collective-permute-start(f32[4,8,1024]{2,1,0:T(8,128)S(1)} %get-tuple-element.46), channel_id=1, source_target_pairs={{0,56},{8,48},{16,40},{24,32},{32,24},{40,16},{48,8},{56,0},{64,12... | collective-permute-start | bytes 393224 | tf_op jit(solution)/shard_map/ppermute | solution.py:419
  17.5 13.3 %collective-permute-start.6 = (f32[4,8,1024]{2,1,0:T(8,128)S(1)}, f32[4,8,1024]{2,1,0:T(8,128)S(1)}, u32[]{:S(2)}, u32[]{:S(2)}) collective-permute-start(f32[4,8,1024]{2,1,0:T(8,128)S(1)} %get-tuple-element.47), channel_id=1, source_target_pairs={{0,48},{8,56},{16,32},{24,40},{32,16},{40,24},{48,0},{56,8},{64,11... | collective-permute-start | bytes 393224 | tf_op jit(solution)/shard_map/ppermute | solution.py:419
  22.4 8.4 %collective-permute-start.7 = (f32[4,8,1024]{2,1,0:T(8,128)S(1)}, f32[4,8,1024]{2,1,0:T(8,128)S(1)}, u32[]{:S(2)}, u32[]{:S(2)}) collective-permute-start(f32[4,8,1024]{2,1,0:T(8,128)S(1)} %get-tuple-element.48), channel_id=1, source_target_pairs={{0,40},{8,32},{16,56},{24,48},{32,8},{40,0},{48,24},{56,16},{64,10... | collective-permute-start | bytes 393224 | tf_op jit(solution)/shard_map/ppermute | solution.py:419
  22.4 8.6 %collective-permute-start.8 = (f32[4,8,1024]{2,1,0:T(8,128)S(1)}, f32[4,8,1024]{2,1,0:T(8,128)S(1)}, u32[]{:S(2)}, u32[]{:S(2)}) collective-permute-start(f32[4,8,1024]{2,1,0:T(8,128)S(1)} %get-tuple-element.49), channel_id=1, source_target_pairs={{0,32},{8,40},{16,48},{24,56},{32,0},{40,8},{48,16},{56,24},{64,96... | collective-permute-start | bytes 393224 | tf_op jit(solution)/shard_map/ppermute | solution.py:419
  27.6 8.5 %collective-permute-start.9 = (f32[4,8,1024]{2,1,0:T(8,128)S(1)}, f32[4,8,1024]{2,1,0:T(8,128)S(1)}, u32[]{:S(2)}, u32[]{:S(2)}) collective-permute-start(f32[4,8,1024]{2,1,0:T(8,128)S(1)} %get-tuple-element.50), channel_id=1, source_target_pairs={{0,24},{8,16},{16,8},{24,0},{32,56},{40,48},{48,40},{56,32},{64,88... | collective-permute-start | bytes 393224 | tf_op jit(solution)/shard_map/ppermute | solution.py:419
  27.6 8.5 %collective-permute-start.10 = (f32[4,8,1024]{2,1,0:T(8,128)S(1)}, f32[4,8,1024]{2,1,0:T(8,128)S(1)}, u32[]{:S(2)}, u32[]{:S(2)}) collective-permute-start(f32[4,8,1024]{2,1,0:T(8,128)S(1)} %get-tuple-element.51), channel_id=1, source_target_pairs={{0,16},{8,24},{16,0},{24,8},{32,48},{40,56},{48,32},{56,40},{64,80... | collective-permute-start | bytes 393224 | tf_op jit(solution)/shard_map/ppermute | solution.py:419
  36.4 6.6 %collective-permute-start.11 = (f32[8,1024]{1,0:T(8,128)S(1)}, f32[8,1024]{1,0:T(8,128)S(1)}, u32[]{:S(2)}, u32[]{:S(2)}) collective-permute-start(f32[8,1024]{1,0:T(8,128)S(1)} %get-tuple-element.54), channel_id=1, source_target_pairs={{0,64},{8,72},{16,80},{24,88},{32,96},{40,104},{48,112},{56,120},{... | collective-permute-start | bytes 98312 | tf_op jit(solution)/shard_map/ppermute | solution.py:419
  36.5 7.9 %collective-permute-start.12 = (f32[8,1024]{1,0:T(8,128)S(1)}, f32[8,1024]{1,0:T(8,128)S(1)}, u32[]{:S(2)}, u32[]{:S(2)}) collective-permute-start(f32[8,1024]{1,0:T(8,128)S(1)} %get-tuple-element.55), channel_id=1, source_target_pairs={{0,128},{8,136},{16,144},{24,152},{32,160},{40,168},{48,176},{56,1... | collective-permute-start | bytes 98312 | tf_op jit(solution)/shard_map/ppermute | solution.py:419
  39.5 6.0 %collective-permute-start.13 = (f32[8,1024]{1,0:T(8,128)S(1)}, f32[8,1024]{1,0:T(8,128)S(1)}, u32[]{:S(2)}, u32[]{:S(2)}) collective-permute-start(f32[8,1024]{1,0:T(8,128)S(1)} %get-tuple-element.56), channel_id=1, source_target_pairs={{0,192},{8,200},{16,208},{24,216},{32,224},{40,232},{48,240},{56,2... | collective-permute-start | bytes 98312 | tf_op jit(solution)/shard_map/ppermute | solution.py:419

commit v3 on v2

--- a/solution.py
+++ b/solution.py
@@ -14,8 +14,8 @@
 LANES = 128
 MIB = 1024 * 1024
 F32 = jnp.float32
-ORDER8 = (1, 7, 6, 5, 4, 3, 2, 0)
-ORDER4 = (1, 2, 3, 0)
+ORDER8 = (1, 7, 6, 5, 3, 4, 2, 0)
+ORDER4 = (2, 3, 1, 0)
 
 
 def params(mib):
@@ -38,12 +38,13 @@
         copy.start()
     copies[4].wait()
     units = (t[...].astype(F32) * UNIT).astype(jnp.int32)
-    for pair in range(2):
-        word = units[2 * pair : 2 * pair + 1] | (units[2 * pair + 1 : 2 * pair + 2] << 16)
-        for half in range(2):
-            table_ref[2 * pair + half] = jnp.broadcast_to(
-                word[:, half * LANES : (half + 1) * LANES], (8, LANES)
-            )
+    red, green, blue, extinction = (units[i : i + 1] for i in range(4))
+    word = red | (green << 12) | (blue << 24)
+    rest = extinction | ((blue >> 8) << 12)
+    halves = slice(0, LANES), slice(LANES, 2 * LANES)
+    parts = [word[:, half] for half in halves] + [rest[:, halves[0]] | (rest[:, halves[1]] << 16)]
+    for i, part in enumerate(parts):
+        table_ref[i] = jnp.broadcast_to(part, (8, LANES))
     copies[2].wait()
     copies[3].wait()
     odd = lat_odd == 1
@@ -64,7 +65,7 @@
             jax.ShapeDtypeStruct((rows, line), F32),
             jax.ShapeDtypeStruct((depth, line), F32),
             jax.ShapeDtypeStruct((depth, line), F32),
-            jax.ShapeDtypeStruct((4, 8, LANES), jnp.int32),
+            jax.ShapeDtypeStruct((3, 8, LANES), jnp.int32),
         ],
         in_specs=[pl.BlockSpec(memory_space=pl.ANY)] * 2,
         out_specs=[pl.BlockSpec(memory_space=pl.ANY)] * 2
@@ -96,36 +97,44 @@
 def look_up(table, bins):
     column = bins & (LANES - 1)
     upper = bins >= LANES
-    values = []
-    for low_half, high_half in table:
-        word = jnp.where(upper, columns_of(high_half, column), columns_of(low_half, column))
-        values += [(word & 0xFFFF).astype(F32), (word >> 16).astype(F32)]
-    return values
+    low_half, high_half, rest = (columns_of(part, column) for part in table)
+    word = jnp.where(upper, high_half, low_half)
+    rest = jnp.where(upper, rest >> 16, rest)
+    blue = ((rest >> 4) & 0xF00) | lax.shift_right_logical(word, 24)
+    units = (word & 0xFFF, (word >> 12) & 0xFFF, blue, rest & 0xFFF)
+    return [value.astype(F32) for value in units]
 
 
 def look_kernel(spacing, d_hbm, b_hbm, o_hbm, t_ref, d_ref, w_ref, l_ref, o_ref, b, sems):
     depth, rows, line = d_hbm.shape
 
-    def copies(t):
-        at = pl.ds(pl.multiple_of(t * 8, 8), 8)
-        inner = pl.ds(pl.multiple_of(t * 8 + 8, 8), 8)
+    cuts = (0, 8, 32, rows)
+
+    def copies(part):
+        first, size = cuts[part], cuts[part + 1] - cuts[part]
+        at, inner = pl.ds(first, size), pl.ds(first + 8, size)
         return [
-            pltpu.make_async_copy(b_hbm.at[:, at], b.at[:, at], sems.at[0, t]),
-            pltpu.make_async_copy(d_hbm.at[:, at], d_ref.at[:, inner], sems.at[1, t]),
-            pltpu.make_async_copy(o_hbm.at[at], o_ref.at[at], sems.at[2, t]),
+            pltpu.make_async_copy(b_hbm.at[:, at], b.at[:, at], sems.at[0, part]),
+            pltpu.make_async_copy(d_hbm.at[:, at], d_ref.at[:, inner], sems.at[1, part]),
+            pltpu.make_async_copy(o_hbm.at[at], o_ref.at[at], sems.at[2, part]),
         ]
 
-    for t in range(rows // 8):
-        for copy in copies(t):
+    for part in range(len(cuts) - 1):
+        for copy in copies(part):
             copy.start()
-    table = [[t_ref[2 * pair + half] for half in range(2)] for pair in range(2)]
+    table = [t_ref[i] for i in range(3)]
     scale = -spacing / (UNIT * math.log(2.0))
 
     def tile(t, carry):
         at = pl.ds(pl.multiple_of(t * 8, 8), 8)
         inner = pl.ds(pl.multiple_of(t * 8 + 8, 8), 8)
-        for copy in copies(t):
-            copy.wait()
+        for part in range(len(cuts) - 1):
+
+            @pl.when(t * 8 == cuts[part])
+            def _(part=part):
+                for copy in copies(part):
+                    copy.wait()
+
         for c in range(line // LANES):
             cols = slice(c * LANES, (c + 1) * LANES)
             reverse = o_ref[at, cols] == 1
@@ -169,7 +178,7 @@
         out_specs=[vmem] * 4,
         scratch_shapes=[
             pltpu.VMEM((depth, rows, line), jnp.int32),
-            pltpu.SemaphoreType.DMA((3, rows // 8)),
+            pltpu.SemaphoreType.DMA((3, 3)),
         ],
         compiler_params=params(12),
         cost_estimate=pl.CostEstimate(
@@ -272,7 +281,7 @@
     return tiles
 
 
-def edges_kernel(d_ref, za_ref, zb_ref, o_ref, c_ref, w_ref, l_ref, a_ref, n_ref, *rest):
+def edges_kernel(d_ref, zb_ref, za_ref, o_ref, c_ref, w_ref, l_ref, a_ref, n_ref, *rest):
     outs, mask_ref, s = rest[:8], rest[8], rest[9]
     depth, line = d_ref.shape[0], d_ref.shape[2]
     slab = lax.axis_index("slab")
@@ -334,7 +343,7 @@
             flops=40 * depth * rows * line, bytes_accessed=4 * depth * rows * line, transcendentals=depth * rows * line
         ),
         name="edges",
-    )(density, za, zb, order, color, weight, light, tilt, norm)
+    )(density, zb, za, order, color, weight, light, tilt, norm)
 
 
 def merge(a, b, b_first):
@@ -420,11 +429,18 @@
 
 
 def swap_odd(block, axis):
-    count = lax.axis_size(axis)
+    slabs, lats = lax.axis_size("slab"), lax.axis_size("lat")
     route = []
-    for i in range(1, count, 2):
-        route += [(i, (i + 1) % count), ((i + 1) % count, i)]
-    return lax.ppermute(block, axis, route)
+    for slab in range(slabs):
+        for lat in range(lats):
+            at, count = (slab, slabs) if axis == "slab" else (lat, lats)
+            step = 2 * (at & 1) - 1
+            if at in (0, count - 1):
+                partner = (slab, lat ^ 1) if axis == "slab" else (slab ^ 1, lat)
+            else:
+                partner = (slab + step, lat) if axis == "slab" else (slab, lat + step)
+            route.append((slab * lats + lat, partner[0] * lats + partner[1]))
+    return lax.ppermute(block, ("slab", "lat"), route)
 
 
 def shards(density, bins, transfer, depth_order):

time: 46.3 us -> 44.1 us (0.952)
  starting transfers between devices: 26.3 us -> 25.4 us
  waiting for transfers between devices: 11.7 us -> 10.9 us
    ppermute x2, starting transfers between devices: 8.12 us -> 0.74 us  [swap_odd(): return lax.ppermute(block, ('slab', 'lat'), route)]
    ppermute x12, starting transfers between devices: 18.2 us -> 24.6 us  [swap(): return lax.ppermute(block, axis, [(i, i ^ step) for i in range(count)])]
    ppermute x12, waiting for transfers between devices: 11.4 us -> 10.9 us  [swap(): return lax.ppermute(block, axis, [(i, i ^ step) for i in range(count)])]
  transfers between devices with their start and end apart: 14 -> 14, of which waited for: 6 -> 9; matrix products, arithmetic and copies ran while one was open for 0% -> 0% of each run, Pallas kernels for 11% -> 10%
where the time goes in v3:
time: 44.1 us; the launch traced here: 44 us
  starting transfers between devices  25.4 us (58%)
  waiting for transfers between devices  10.9 us (25%)
  Pallas kernels  7.67 us (17%)
    ppermute x12, starting transfers between devices, swap(): return lax.ppermute(block, axis, [(i, i ^ step) for i in range(count)])  24.6 us
    ppermute x12, waiting for transfers between devices, swap(): return lax.ppermute(block, axis, [(i, i ^ step) for i in range(count)])  10.9 us
    pallas_call x1, Pallas kernels, look(): pl.pallas_call(lambda *refs: look_kernel(spacing, *refs), out_shape=[jax....  3.42 us
    pallas_call x1, Pallas kernels, faces(): pl.pallas_call(faces_kernel, out_shape=[jax.ShapeDtypeStruct((rows, line)...  1.15 us
    pallas_call x1, Pallas kernels, slopes(): pl.pallas_call(slopes_kernel, out_shape=[jax.ShapeDtypeStruct(density.sha...  1.15 us
    pallas_call x1, Pallas kernels, edges(): pl.pallas_call(edges_kernel, out_shape=[jax.ShapeDtypeStruct((4, 8, line)...  0.99 us
  transfers between devices with their start and end apart: 14, of which 9 were waited for; matrix products, arithmetic and copies ran while one was open for 0% of the time, Pallas kernels for 10%

profile of v3, /device:TPU:2, one launch (start us, length us, event | category | flops | bytes accessed | tf_op | source)
XLA Modules:
  0.0 44.0 jit_solution(17207029909239836338)
XLA Ops:
  0.0 1.2 %faces.1 = (f32[64,1024]{1,0:T(8,128)S(1)}, f32[64,1024]{1,0:T(8,128)S(1)}, f32[4,1024]{1,0:T(4,128)S(1)}, f32[4,1024]{1,0:T(4,128)S(1)}, s32[3,8,128]{2,1,0:T(8,128)S(1)}) custom-call(f32[4,64,1024]{2,1,0:T(8,128)} %refs_0_.1, bf16[4,256]{1,0:T(4,128)(2,1)} %t_ref.1), custom_call_target="tpu_custom_call" | custom-call | tf_op jit(solution)/shard_map/faces/pallas_call | solution.py:61
  1.2 0.1 collective-permute-start.2
  1.3 3.1 %collective-permute-start.3 = (f32[64,1024]{1,0:T(8,128)S(1)}, f32[64,1024]{1,0:T(8,128)S(1)}, u32[]{:S(2)}, u32[]{:S(2)}) collective-permute-start(f32[64,1024]{1,0:T(8,128)S(1)} %get-tuple-element.39), channel_id=1, source_target_pairs={{0,8},{8,0},{16,24},{24,16},{32,40},{40,32},{48,56},{56,48},{64,72... | collective-permute-start | bytes 786440 | tf_op jit(solution)/shard_map/ppermute | solution.py:428
  4.4 0.0 collective-permute-start
  4.4 0.6 %collective-permute-start.1 = (f32[4,1024]{1,0:T(4,128)S(1)}, f32[4,1024]{1,0:T(4,128)S(1)}, u32[]{:S(2)}, u32[]{:S(2)}) collective-permute-start(f32[4,1024]{1,0:T(4,128)S(1)} %get-tuple-element.36), channel_id=1, source_target_pairs={{0,8},{1,2},{2,1},{3,4},{4,3},{5,6},{6,5},{7,15},{8,0},{9,10},{10,... | collective-permute-start | bytes 49160 | tf_op jit(solution)/shard_map/ppermute | solution.py:443
  5.1 3.4 %look.1 = (f32[4,80,1024]{2,1,0:T(8,128)S(1)}, f32[4,3,64,1024]{3,2,1,0:T(8,128)S(1)}, f32[64,1024]{1,0:T(8,128)S(1)}, s32[64,1024]{1,0:T(8,128)S(1)}) custom-call(f32[4,64,1024]{2,1,0:T(8,128)} %refs_0_.1, s32[4,64,1024]{2,1,0:T(8,128)} %refs_1_.1, s32[64,1024]{1,0:T(8,128)} %refs_2_.1, s32[3,8,128]{2,1,0:T(8,128)S(1)} %get-tuple-element.32.refs_3_), custom_call_target="tpu_custom_call" | custom-call | flops 13107200 | bytes 3145728 | tf_op jit(solution)/shard_map/look/pallas_call | solution.py:169
  8.5 0.0 collective-permute-done.ya_ref
  8.5 0.0 collective-permute-done.1.yb_ref
  8.5 1.2 %slopes.1 = (f32[4,80,1024]{2,1,0:T(8,128)S(1)}, f32[3,64,1024]{2,1,0:T(8,128)S(1)}, f32[2,64,1024]{2,1,0:T(8,128)S(1)}, f32[2,64,1024]{2,1,0:T(8,128)S(1)}) custom-call(f32[4,80,1024]{2,1,0:T(8,128)S(1)} %get-tuple-element.33.d_in, f32[4,3,64,1024]{3,2,1,0:T(8,128)S(1)} %get-tuple-element.34.w_ref, ...), custom_call_target="tpu_custom_call", output_to_operand_aliasing={{0}: (0, {})} | custom-call | flops 13107200 | bytes 3145728 | tf_op jit(solution)/shard_map/slopes/pallas_call | solution.py:251
  9.7 0.0 collective-permute-done.2.zb_ref
  9.7 0.7 %collective-permute-done.3.za_ref = f32[64,1024]{1,0:T(8,128)S(1)} collective-permute-done((f32[64,1024]{1,0:T(8,128)S(1)}, f32[64,1024]{1,0:T(8,128)S(1)}, u32[]{:S(2)}, u32[]{:S(2)}) %collective-permute-start.3) | collective-permute-done | bytes 262176 | tf_op jit(solution)/shard_map/ppermute | solution.py:428
  10.4 1.0 %edges.1 = (f32[4,8,1024]{2,1,0:T(8,128)S(1)}, f32[4,8,1024]{2,1,0:T(8,128)S(1)}, f32[4,8,1024]{2,1,0:T(8,128)S(1)}, f32[4,8,1024]{2,1,0:T(8,128)S(1)}, f32[4,8,...) custom-call(f32[4,80,1024]{2,1,0:T(8,128)S(1)} %get-tuple-element.37, ...), custom_call_target="tpu_custom_call" | custom-call | flops 10485760 | bytes 1048576 | tf_op jit(solution)/shard_map/edges/pallas_call | solution.py:334
  11.4 1.8 %collective-permute-start.4 = (f32[4,8,1024]{2,1,0:T(8,128)S(1)}, f32[4,8,1024]{2,1,0:T(8,128)S(1)}, u32[]{:S(2)}, u32[]{:S(2)}) collective-permute-start(f32[4,8,1024]{2,1,0:T(8,128)S(1)} %get-tuple-element.45), channel_id=1, source_target_pairs={{0,8},{8,0},{16,24},{24,16},{32,40},{40,32},{48,56},{56,48},{64,72... | collective-permute-start | bytes 393224 | tf_op jit(solution)/shard_map/ppermute | solution.py:428
  13.3 3.7 %collective-permute-start.5 = (f32[4,8,1024]{2,1,0:T(8,128)S(1)}, f32[4,8,1024]{2,1,0:T(8,128)S(1)}, u32[]{:S(2)}, u32[]{:S(2)}) collective-permute-start(f32[4,8,1024]{2,1,0:T(8,128)S(1)} %get-tuple-element.46), channel_id=1, source_target_pairs={{0,56},{8,48},{16,40},{24,32},{32,24},{40,16},{48,8},{56,0},{64,12... | collective-permute-start | bytes 393224 | tf_op jit(solution)/shard_map/ppermute | solution.py:428
  17.0 1.4 %collective-permute-start.6 = (f32[4,8,1024]{2,1,0:T(8,128)S(1)}, f32[4,8,1024]{2,1,0:T(8,128)S(1)}, u32[]{:S(2)}, u32[]{:S(2)}) collective-permute-start(f32[4,8,1024]{2,1,0:T(8,128)S(1)} %get-tuple-element.47), channel_id=1, source_target_pairs={{0,48},{8,56},{16,32},{24,40},{32,16},{40,24},{48,0},{56,8},{64,11... | collective-permute-start | bytes 393224 | tf_op jit(solution)/shard_map/ppermute | solution.py:428
  18.3 1.3 %collective-permute-start.7 = (f32[4,8,1024]{2,1,0:T(8,128)S(1)}, f32[4,8,1024]{2,1,0:T(8,128)S(1)}, u32[]{:S(2)}, u32[]{:S(2)}) collective-permute-start(f32[4,8,1024]{2,1,0:T(8,128)S(1)} %get-tuple-element.48), channel_id=1, source_target_pairs={{0,40},{8,32},{16,56},{24,48},{32,8},{40,0},{48,24},{56,16},{64,10... | collective-permute-start | bytes 393224 | tf_op jit(solution)/shard_map/ppermute | solution.py:428
  19.6 2.4 %collective-permute-start.8 = (f32[4,8,1024]{2,1,0:T(8,128)S(1)}, f32[4,8,1024]{2,1,0:T(8,128)S(1)}, u32[]{:S(2)}, u32[]{:S(2)}) collective-permute-start(f32[4,8,1024]{2,1,0:T(8,128)S(1)} %get-tuple-element.49), channel_id=1, source_target_pairs={{0,24},{8,16},{16,8},{24,0},{32,56},{40,48},{48,40},{56,32},{64,88... | collective-permute-start | bytes 393224 | tf_op jit(solution)/shard_map/ppermute | solution.py:428
  22.0 0.0 collective-permute-done.4.refs_0_
  22.0 0.5 %collective-permute-start.9 = (f32[4,8,1024]{2,1,0:T(8,128)S(1)}, f32[4,8,1024]{2,1,0:T(8,128)S(1)}, u32[]{:S(2)}, u32[]{:S(2)}) collective-permute-start(f32[4,8,1024]{2,1,0:T(8,128)S(1)} %get-tuple-element.50), channel_id=1, source_target_pairs={{0,32},{8,40},{16,48},{24,56},{32,0},{40,8},{48,16},{56,24},{64,96... | collective-permute-start | bytes 393224 | tf_op jit(solution)/shard_map/ppermute | solution.py:428
  22.4 0.0 collective-permute-done.5.refs_1_
  22.4 1.7 %collective-permute-start.10 = (f32[4,8,1024]{2,1,0:T(8,128)S(1)}, f32[4,8,1024]{2,1,0:T(8,128)S(1)}, u32[]{:S(2)}, u32[]{:S(2)}) collective-permute-start(f32[4,8,1024]{2,1,0:T(8,128)S(1)} %get-tuple-element.51), channel_id=1, source_target_pairs={{0,16},{8,24},{16,0},{24,8},{32,48},{40,56},{48,32},{56,40},{64,80... | collective-permute-start | bytes 393224 | tf_op jit(solution)/shard_map/ppermute | solution.py:428
  24.1 1.8 %collective-permute-done.6.refs_2_ = f32[4,8,1024]{2,1,0:T(8,128)S(1)} collective-permute-done((f32[4,8,1024]{2,1,0:T(8,128)S(1)}, f32[4,8,1024]{2,1,0:T(8,128)S(1)}, u32[]{:S(2)}, u32[]{:S(2)}) %collective-permute-start.6) | collective-permute-done | bytes 131104 | tf_op jit(solution)/shard_map/ppermute | solution.py:428
  25.9 1.8 %collective-permute-done.7.refs_3_ = f32[4,8,1024]{2,1,0:T(8,128)S(1)} collective-permute-done((f32[4,8,1024]{2,1,0:T(8,128)S(1)}, f32[4,8,1024]{2,1,0:T(8,128)S(1)}, u32[]{:S(2)}, u32[]{:S(2)}) %collective-permute-start.7) | collective-permute-done | bytes 131104 | tf_op jit(solution)/shard_map/ppermute | solution.py:428
  27.7 0.6 %collective-permute-done.8.refs_4_ = f32[4,8,1024]{2,1,0:T(8,128)S(1)} collective-permute-done((f32[4,8,1024]{2,1,0:T(8,128)S(1)}, f32[4,8,1024]{2,1,0:T(8,128)S(1)}, u32[]{:S(2)}, u32[]{:S(2)}) %collective-permute-start.8) | collective-permute-done | bytes 131104 | tf_op jit(solution)/shard_map/ppermute | solution.py:428
  28.3 0.2 collective-permute-done.9.refs_5_
  28.5 1.2 %collective-permute-done.10.refs_6_ = f32[4,8,1024]{2,1,0:T(8,128)S(1)} collective-permute-done((f32[4,8,1024]{2,1,0:T(8,128)S(1)}, f32[4,8,1024]{2,1,0:T(8,128)S(1)}, u32[]{:S(2)}, u32[]{:S(2)}) %collective-permute-start.10) | collective-permute-done | bytes 131104 | tf_op jit(solution)/shard_map/ppermute | solution.py:428
  29.7 0.3 merge_eight.1
  30.0 7.2 %collective-permute-start.11 = (f32[8,1024]{1,0:T(8,128)S(1)}, f32[8,1024]{1,0:T(8,128)S(1)}, u32[]{:S(2)}, u32[]{:S(2)}) collective-permute-start(f32[8,1024]{1,0:T(8,128)S(1)} %get-tuple-element.54), channel_id=1, source_target_pairs={{0,128},{8,136},{16,144},{24,152},{32,160},{40,168},{48,176},{56,1... | collective-permute-start | bytes 98312 | tf_op jit(solution)/shard_map/ppermute | solution.py:428
  37.1 1.0 %collective-permute-start.12 = (f32[8,1024]{1,0:T(8,128)S(1)}, f32[8,1024]{1,0:T(8,128)S(1)}, u32[]{:S(2)}, u32[]{:S(2)}) collective-permute-start(f32[8,1024]{1,0:T(8,128)S(1)} %get-tuple-element.55), channel_id=1, source_target_pairs={{0,192},{8,200},{16,208},{24,216},{32,224},{40,232},{48,240},{56,2... | collective-permute-start | bytes 98312 | tf_op jit(solution)/shard_map/ppermute | solution.py:428
  38.1 0.6 %collective-permute-start.13 = (f32[8,1024]{1,0:T(8,128)S(1)}, f32[8,1024]{1,0:T(8,128)S(1)}, u32[]{:S(2)}, u32[]{:S(2)}) collective-permute-start(f32[8,1024]{1,0:T(8,128)S(1)} %get-tuple-element.56), channel_id=1, source_target_pairs={{0,64},{8,72},{16,80},{24,88},{32,96},{40,104},{48,112},{56,120},{... | collective-permute-start | bytes 98312 | tf_op jit(solution)/shard_map/ppermute | solution.py:428
  38.8 0.5 %collective-permute-done.11.refs_0_ = f32[8,1024]{1,0:T(8,128)S(1)} collective-permute-done((f32[8,1024]{1,0:T(8,128)S(1)}, f32[8,1024]{1,0:T(8,128)S(1)}, u32[]{:S(2)}, u32[]{:S(2)}) %collective-permute-start.11) | collective-permute-done | bytes 32800 | tf_op jit(solution)/shard_map/ppermute | solution.py:428
  39.3 4.0 %collective-permute-done.12.refs_1_ = f32[8,1024]{1,0:T(8,128)S(1)} collective-permute-done((f32[8,1024]{1,0:T(8,128)S(1)}, f32[8,1024]{1,0:T(8,128)S(1)}, u32[]{:S(2)}, u32[]{:S(2)}) %collective-permute-start.12) | collective-permute-done | bytes 32800 | tf_op jit(solution)/shard_map/ppermute | solution.py:428
  43.2 0.1 collective-permute-done.13.refs_2_
  43.3 0.7 %merge_four.1 = f32[4,2,1024]{2,1,0:T(2,128)} custom-call(f32[8,1024]{1,0:T(8,128)S(1)} %collective-permute-done.11.refs_0_, f32[8,1024]{1,0:T(8,128)S(1)} %collective-permute-done.12.refs_1_, f32[8,1024]{1,0:T(8,128)S(1)} %collective-permute-done.13.refs_2_, f32[8,1024]{1,0:T(8,128)S(1)} %get-tuple-element.57.refs_3_, f32[8,1024]{1,0:T(8,128)S(1)} %get-tuple-element.58.refs_4_), custom_call_target="tpu_custom_call" | custom-call | tf_op jit(solution)/shard_map/merge_four/pallas_call | solution.py:416
Async XLA Ops:
  1.2 8.5 %collective-permute-start.2 = (f32[64,1024]{1,0:T(8,128)S(1)}, f32[64,1024]{1,0:T(8,128)S(1)}, u32[]{:S(2)}, u32[]{:S(2)}) collective-permute-start(f32[64,1024]{1,0:T(8,128)S(1)} %get-tuple-element.38), channel_id=1, source_target_pairs={{0,1},{1,0},{2,3},{3,2},{4,5},{5,4},{6,7},{7,6},{8,16},{9,17},{10,... | collective-permute-start | bytes 786440 | tf_op jit(solution)/shard_map/ppermute | solution.py:443
  1.3 9.2 %collective-permute-start.3 = (f32[64,1024]{1,0:T(8,128)S(1)}, f32[64,1024]{1,0:T(8,128)S(1)}, u32[]{:S(2)}, u32[]{:S(2)}) collective-permute-start(f32[64,1024]{1,0:T(8,128)S(1)} %get-tuple-element.39), channel_id=1, source_target_pairs={{0,8},{8,0},{16,24},{24,16},{32,40},{40,32},{48,56},{56,48},{64,72... | collective-permute-start | bytes 786440 | tf_op jit(solution)/shard_map/ppermute | solution.py:428
  4.4 4.1 %collective-permute-start = (f32[4,1024]{1,0:T(4,128)S(1)}, f32[4,1024]{1,0:T(4,128)S(1)}, u32[]{:S(2)}, u32[]{:S(2)}) collective-permute-start(f32[4,1024]{1,0:T(4,128)S(1)} %get-tuple-element.35), channel_id=1, source_target_pairs={{0,1},{1,0},{2,3},{3,2},{4,5},{5,4},{6,7},{7,6},{8,9},{9,8},{10,11... | collective-permute-start | bytes 49160 | tf_op jit(solution)/shard_map/ppermute | solution.py:428
  4.4 4.1 %collective-permute-start.1 = (f32[4,1024]{1,0:T(4,128)S(1)}, f32[4,1024]{1,0:T(4,128)S(1)}, u32[]{:S(2)}, u32[]{:S(2)}) collective-permute-start(f32[4,1024]{1,0:T(4,128)S(1)} %get-tuple-element.36), channel_id=1, source_target_pairs={{0,8},{1,2},{2,1},{3,4},{4,3},{5,6},{6,5},{7,15},{8,0},{9,10},{10,... | collective-permute-start | bytes 49160 | tf_op jit(solution)/shard_map/ppermute | solution.py:443
  11.4 10.5 %collective-permute-start.4 = (f32[4,8,1024]{2,1,0:T(8,128)S(1)}, f32[4,8,1024]{2,1,0:T(8,128)S(1)}, u32[]{:S(2)}, u32[]{:S(2)}) collective-permute-start(f32[4,8,1024]{2,1,0:T(8,128)S(1)} %get-tuple-element.45), channel_id=1, source_target_pairs={{0,8},{8,0},{16,24},{24,16},{32,40},{40,32},{48,56},{56,48},{64,72... | collective-permute-start | bytes 393224 | tf_op jit(solution)/shard_map/ppermute | solution.py:428
  13.3 9.2 %collective-permute-start.5 = (f32[4,8,1024]{2,1,0:T(8,128)S(1)}, f32[4,8,1024]{2,1,0:T(8,128)S(1)}, u32[]{:S(2)}, u32[]{:S(2)}) collective-permute-start(f32[4,8,1024]{2,1,0:T(8,128)S(1)} %get-tuple-element.46), channel_id=1, source_target_pairs={{0,56},{8,48},{16,40},{24,32},{32,24},{40,16},{48,8},{56,0},{64,12... | collective-permute-start | bytes 393224 | tf_op jit(solution)/shard_map/ppermute | solution.py:428
  17.0 8.9 %collective-permute-start.6 = (f32[4,8,1024]{2,1,0:T(8,128)S(1)}, f32[4,8,1024]{2,1,0:T(8,128)S(1)}, u32[]{:S(2)}, u32[]{:S(2)}) collective-permute-start(f32[4,8,1024]{2,1,0:T(8,128)S(1)} %get-tuple-element.47), channel_id=1, source_target_pairs={{0,48},{8,56},{16,32},{24,40},{32,16},{40,24},{48,0},{56,8},{64,11... | collective-permute-start | bytes 393224 | tf_op jit(solution)/shard_map/ppermute | solution.py:428
  18.3 9.3 %collective-permute-start.7 = (f32[4,8,1024]{2,1,0:T(8,128)S(1)}, f32[4,8,1024]{2,1,0:T(8,128)S(1)}, u32[]{:S(2)}, u32[]{:S(2)}) collective-permute-start(f32[4,8,1024]{2,1,0:T(8,128)S(1)} %get-tuple-element.48), channel_id=1, source_target_pairs={{0,40},{8,32},{16,56},{24,48},{32,8},{40,0},{48,24},{56,16},{64,10... | collective-permute-start | bytes 393224 | tf_op jit(solution)/shard_map/ppermute | solution.py:428
  19.6 8.7 %collective-permute-start.8 = (f32[4,8,1024]{2,1,0:T(8,128)S(1)}, f32[4,8,1024]{2,1,0:T(8,128)S(1)}, u32[]{:S(2)}, u32[]{:S(2)}) collective-permute-start(f32[4,8,1024]{2,1,0:T(8,128)S(1)} %get-tuple-element.49), channel_id=1, source_target_pairs={{0,24},{8,16},{16,8},{24,0},{32,56},{40,48},{48,40},{56,32},{64,88... | collective-permute-start | bytes 393224 | tf_op jit(solution)/shard_map/ppermute | solution.py:428
  22.0 6.5 %collective-permute-start.9 = (f32[4,8,1024]{2,1,0:T(8,128)S(1)}, f32[4,8,1024]{2,1,0:T(8,128)S(1)}, u32[]{:S(2)}, u32[]{:S(2)}) collective-permute-start(f32[4,8,1024]{2,1,0:T(8,128)S(1)} %get-tuple-element.50), channel_id=1, source_target_pairs={{0,32},{8,40},{16,48},{24,56},{32,0},{40,8},{48,16},{56,24},{64,96... | collective-permute-start | bytes 393224 | tf_op jit(solution)/shard_map/ppermute | solution.py:428
  22.4 7.3 %collective-permute-start.10 = (f32[4,8,1024]{2,1,0:T(8,128)S(1)}, f32[4,8,1024]{2,1,0:T(8,128)S(1)}, u32[]{:S(2)}, u32[]{:S(2)}) collective-permute-start(f32[4,8,1024]{2,1,0:T(8,128)S(1)} %get-tuple-element.51), channel_id=1, source_target_pairs={{0,16},{8,24},{16,0},{24,8},{32,48},{40,56},{48,32},{56,40},{64,80... | collective-permute-start | bytes 393224 | tf_op jit(solution)/shard_map/ppermute | solution.py:428
  30.0 9.3 %collective-permute-start.11 = (f32[8,1024]{1,0:T(8,128)S(1)}, f32[8,1024]{1,0:T(8,128)S(1)}, u32[]{:S(2)}, u32[]{:S(2)}) collective-permute-start(f32[8,1024]{1,0:T(8,128)S(1)} %get-tuple-element.54), channel_id=1, source_target_pairs={{0,128},{8,136},{16,144},{24,152},{32,160},{40,168},{48,176},{56,1... | collective-permute-start | bytes 98312 | tf_op jit(solution)/shard_map/ppermute | solution.py:428
  37.1 6.1 %collective-permute-start.12 = (f32[8,1024]{1,0:T(8,128)S(1)}, f32[8,1024]{1,0:T(8,128)S(1)}, u32[]{:S(2)}, u32[]{:S(2)}) collective-permute-start(f32[8,1024]{1,0:T(8,128)S(1)} %get-tuple-element.55), channel_id=1, source_target_pairs={{0,192},{8,200},{16,208},{24,216},{32,224},{40,232},{48,240},{56,2... | collective-permute-start | bytes 98312 | tf_op jit(solution)/shard_map/ppermute | solution.py:428
  38.1 5.2 %collective-permute-start.13 = (f32[8,1024]{1,0:T(8,128)S(1)}, f32[8,1024]{1,0:T(8,128)S(1)}, u32[]{:S(2)}, u32[]{:S(2)}) collective-permute-start(f32[8,1024]{1,0:T(8,128)S(1)} %get-tuple-element.56), channel_id=1, source_target_pairs={{0,64},{8,72},{16,80},{24,88},{32,96},{40,104},{48,112},{56,120},{... | collective-permute-start | bytes 98312 | tf_op jit(solution)/shard_map/ppermute | solution.py:428

commit v4 on v3

--- a/solution.py
+++ b/solution.py
@@ -14,7 +14,7 @@
 LANES = 128
 MIB = 1024 * 1024
 F32 = jnp.float32
-ORDER8 = (1, 7, 6, 5, 3, 4, 2, 0)
+ORDER8 = (1, 7, 3, 5, 2, 6, 4, 0)
 ORDER4 = (2, 3, 1, 0)
 
 

time: 44.1 us -> 44 us (level)
  starting transfers between devices: 25.4 us -> 24.3 us
  waiting for transfers between devices: 10.9 us -> 11.5 us
    ppermute x12, starting transfers between devices: 24.6 us -> 23.5 us  [swap(): return lax.ppermute(block, axis, [(i, i ^ step) for i in range(count)])]
    ppermute x12, waiting for transfers between devices: 10.9 us -> 11.5 us  [swap(): return lax.ppermute(block, axis, [(i, i ^ step) for i in range(count)])]
  transfers between devices with their start and end apart: 14 -> 14, of which waited for: 9 -> 6; matrix products, arithmetic and copies ran while one was open for 0% -> 0% of each run, Pallas kernels for 10% -> 11%
where the time goes in v4:
time: 44 us; the launch traced here: 43.5 us
  starting transfers between devices  24.3 us (55%)
  waiting for transfers between devices  11.5 us (26%)
  Pallas kernels  7.68 us (17%)
    ppermute x12, starting transfers between devices, swap(): return lax.ppermute(block, axis, [(i, i ^ step) for i in range(count)])  23.5 us
    ppermute x12, waiting for transfers between devices, swap(): return lax.ppermute(block, axis, [(i, i ^ step) for i in range(count)])  11.5 us
    pallas_call x1, Pallas kernels, look(): pl.pallas_call(lambda *refs: look_kernel(spacing, *refs), out_shape=[jax....  3.42 us
    pallas_call x1, Pallas kernels, faces(): pl.pallas_call(faces_kernel, out_shape=[jax.ShapeDtypeStruct((rows, line)...  1.15 us
    pallas_call x1, Pallas kernels, slopes(): pl.pallas_call(slopes_kernel, out_shape=[jax.ShapeDtypeStruct(density.sha...  1.15 us
    pallas_call x1, Pallas kernels, edges(): pl.pallas_call(edges_kernel, out_shape=[jax.ShapeDtypeStruct((4, 8, line)...  0.99 us
  transfers between devices with their start and end apart: 14, of which 6 were waited for; matrix products, arithmetic and copies ran while one was open for 0% of the time, Pallas kernels for 11%

profile of v4, /device:TPU:2, one launch (start us, length us, event | category | flops | bytes accessed | tf_op | source)
XLA Modules:
  0.0 43.5 jit_solution(11191916658475338155)
XLA Ops:
  0.0 1.2 %faces.1 = (f32[64,1024]{1,0:T(8,128)S(1)}, f32[64,1024]{1,0:T(8,128)S(1)}, f32[4,1024]{1,0:T(4,128)S(1)}, f32[4,1024]{1,0:T(4,128)S(1)}, s32[3,8,128]{2,1,0:T(8,128)S(1)}) custom-call(f32[4,64,1024]{2,1,0:T(8,128)} %refs_0_.1, bf16[4,256]{1,0:T(4,128)(2,1)} %t_ref.1), custom_call_target="tpu_custom_call" | custom-call | tf_op jit(solution)/shard_map/faces/pallas_call | solution.py:61
  1.2 0.1 collective-permute-start.2
  1.3 3.1 %collective-permute-start.3 = (f32[64,1024]{1,0:T(8,128)S(1)}, f32[64,1024]{1,0:T(8,128)S(1)}, u32[]{:S(2)}, u32[]{:S(2)}) collective-permute-start(f32[64,1024]{1,0:T(8,128)S(1)} %get-tuple-element.39), channel_id=1, source_target_pairs={{0,8},{8,0},{16,24},{24,16},{32,40},{40,32},{48,56},{56,48},{64,72... | collective-permute-start | bytes 786440 | tf_op jit(solution)/shard_map/ppermute | solution.py:428
  4.4 0.0 collective-permute-start
  4.4 0.6 %collective-permute-start.1 = (f32[4,1024]{1,0:T(4,128)S(1)}, f32[4,1024]{1,0:T(4,128)S(1)}, u32[]{:S(2)}, u32[]{:S(2)}) collective-permute-start(f32[4,1024]{1,0:T(4,128)S(1)} %get-tuple-element.36), channel_id=1, source_target_pairs={{0,8},{1,2},{2,1},{3,4},{4,3},{5,6},{6,5},{7,15},{8,0},{9,10},{10,... | collective-permute-start | bytes 49160 | tf_op jit(solution)/shard_map/ppermute | solution.py:443
  5.1 3.4 %look.1 = (f32[4,80,1024]{2,1,0:T(8,128)S(1)}, f32[4,3,64,1024]{3,2,1,0:T(8,128)S(1)}, f32[64,1024]{1,0:T(8,128)S(1)}, s32[64,1024]{1,0:T(8,128)S(1)}) custom-call(f32[4,64,1024]{2,1,0:T(8,128)} %refs_0_.1, s32[4,64,1024]{2,1,0:T(8,128)} %refs_1_.1, s32[64,1024]{1,0:T(8,128)} %refs_2_.1, s32[3,8,128]{2,1,0:T(8,128)S(1)} %get-tuple-element.32.refs_3_), custom_call_target="tpu_custom_call" | custom-call | flops 13107200 | bytes 3145728 | tf_op jit(solution)/shard_map/look/pallas_call | solution.py:169
  8.5 0.0 collective-permute-done.ya_ref
  8.5 0.0 collective-permute-done.1.yb_ref
  8.5 1.2 %slopes.1 = (f32[4,80,1024]{2,1,0:T(8,128)S(1)}, f32[3,64,1024]{2,1,0:T(8,128)S(1)}, f32[2,64,1024]{2,1,0:T(8,128)S(1)}, f32[2,64,1024]{2,1,0:T(8,128)S(1)}) custom-call(f32[4,80,1024]{2,1,0:T(8,128)S(1)} %get-tuple-element.33.d_in, f32[4,3,64,1024]{3,2,1,0:T(8,128)S(1)} %get-tuple-element.34.w_ref, ...), custom_call_target="tpu_custom_call", output_to_operand_aliasing={{0}: (0, {})} | custom-call | flops 13107200 | bytes 3145728 | tf_op jit(solution)/shard_map/slopes/pallas_call | solution.py:251
  9.7 0.0 collective-permute-done.2.zb_ref
  9.7 0.7 %collective-permute-done.3.za_ref = f32[64,1024]{1,0:T(8,128)S(1)} collective-permute-done((f32[64,1024]{1,0:T(8,128)S(1)}, f32[64,1024]{1,0:T(8,128)S(1)}, u32[]{:S(2)}, u32[]{:S(2)}) %collective-permute-start.3) | collective-permute-done | bytes 262176 | tf_op jit(solution)/shard_map/ppermute | solution.py:428
  10.4 1.0 %edges.1 = (f32[4,8,1024]{2,1,0:T(8,128)S(1)}, f32[4,8,1024]{2,1,0:T(8,128)S(1)}, f32[4,8,1024]{2,1,0:T(8,128)S(1)}, f32[4,8,1024]{2,1,0:T(8,128)S(1)}, f32[4,8,...) custom-call(f32[4,80,1024]{2,1,0:T(8,128)S(1)} %get-tuple-element.37, ...), custom_call_target="tpu_custom_call" | custom-call | flops 10485760 | bytes 1048576 | tf_op jit(solution)/shard_map/edges/pallas_call | solution.py:334
  11.4 1.8 %collective-permute-start.4 = (f32[4,8,1024]{2,1,0:T(8,128)S(1)}, f32[4,8,1024]{2,1,0:T(8,128)S(1)}, u32[]{:S(2)}, u32[]{:S(2)}) collective-permute-start(f32[4,8,1024]{2,1,0:T(8,128)S(1)} %get-tuple-element.45), channel_id=1, source_target_pairs={{0,8},{8,0},{16,24},{24,16},{32,40},{40,32},{48,56},{56,48},{64,72... | collective-permute-start | bytes 393224 | tf_op jit(solution)/shard_map/ppermute | solution.py:428
  13.3 3.7 %collective-permute-start.5 = (f32[4,8,1024]{2,1,0:T(8,128)S(1)}, f32[4,8,1024]{2,1,0:T(8,128)S(1)}, u32[]{:S(2)}, u32[]{:S(2)}) collective-permute-start(f32[4,8,1024]{2,1,0:T(8,128)S(1)} %get-tuple-element.46), channel_id=1, source_target_pairs={{0,56},{8,48},{16,40},{24,32},{32,24},{40,16},{48,8},{56,0},{64,12... | collective-permute-start | bytes 393224 | tf_op jit(solution)/shard_map/ppermute | solution.py:428
  17.0 0.9 %collective-permute-start.6 = (f32[4,8,1024]{2,1,0:T(8,128)S(1)}, f32[4,8,1024]{2,1,0:T(8,128)S(1)}, u32[]{:S(2)}, u32[]{:S(2)}) collective-permute-start(f32[4,8,1024]{2,1,0:T(8,128)S(1)} %get-tuple-element.47), channel_id=1, source_target_pairs={{0,24},{8,16},{16,8},{24,0},{32,56},{40,48},{48,40},{56,32},{64,88... | collective-permute-start | bytes 393224 | tf_op jit(solution)/shard_map/ppermute | solution.py:428
  17.8 0.4 %collective-permute-start.7 = (f32[4,8,1024]{2,1,0:T(8,128)S(1)}, f32[4,8,1024]{2,1,0:T(8,128)S(1)}, u32[]{:S(2)}, u32[]{:S(2)}) collective-permute-start(f32[4,8,1024]{2,1,0:T(8,128)S(1)} %get-tuple-element.48), channel_id=1, source_target_pairs={{0,40},{8,32},{16,56},{24,48},{32,8},{40,0},{48,24},{56,16},{64,10... | collective-permute-start | bytes 393224 | tf_op jit(solution)/shard_map/ppermute | solution.py:428
  18.3 2.9 %collective-permute-start.8 = (f32[4,8,1024]{2,1,0:T(8,128)S(1)}, f32[4,8,1024]{2,1,0:T(8,128)S(1)}, u32[]{:S(2)}, u32[]{:S(2)}) collective-permute-start(f32[4,8,1024]{2,1,0:T(8,128)S(1)} %get-tuple-element.49), channel_id=1, source_target_pairs={{0,16},{8,24},{16,0},{24,8},{32,48},{40,56},{48,32},{56,40},{64,80... | collective-permute-start | bytes 393224 | tf_op jit(solution)/shard_map/ppermute | solution.py:428
  21.2 0.0 collective-permute-done.4.refs_0_
  21.2 1.5 %collective-permute-start.9 = (f32[4,8,1024]{2,1,0:T(8,128)S(1)}, f32[4,8,1024]{2,1,0:T(8,128)S(1)}, u32[]{:S(2)}, u32[]{:S(2)}) collective-permute-start(f32[4,8,1024]{2,1,0:T(8,128)S(1)} %get-tuple-element.50), channel_id=1, source_target_pairs={{0,48},{8,56},{16,32},{24,40},{32,16},{40,24},{48,0},{56,8},{64,11... | collective-permute-start | bytes 393224 | tf_op jit(solution)/shard_map/ppermute | solution.py:428
  22.7 0.0 collective-permute-done.5.refs_1_
  22.7 0.8 %collective-permute-start.10 = (f32[4,8,1024]{2,1,0:T(8,128)S(1)}, f32[4,8,1024]{2,1,0:T(8,128)S(1)}, u32[]{:S(2)}, u32[]{:S(2)}) collective-permute-start(f32[4,8,1024]{2,1,0:T(8,128)S(1)} %get-tuple-element.51), channel_id=1, source_target_pairs={{0,32},{8,40},{16,48},{24,56},{32,0},{40,8},{48,16},{56,24},{64,96... | collective-permute-start | bytes 393224 | tf_op jit(solution)/shard_map/ppermute | solution.py:428
  23.5 1.8 %collective-permute-done.6.refs_2_ = f32[4,8,1024]{2,1,0:T(8,128)S(1)} collective-permute-done((f32[4,8,1024]{2,1,0:T(8,128)S(1)}, f32[4,8,1024]{2,1,0:T(8,128)S(1)}, u32[]{:S(2)}, u32[]{:S(2)}) %collective-permute-start.6) | collective-permute-done | bytes 131104 | tf_op jit(solution)/shard_map/ppermute | solution.py:428
  25.2 0.0 collective-permute-done.7.refs_3_
  25.3 3.6 %collective-permute-done.8.refs_4_ = f32[4,8,1024]{2,1,0:T(8,128)S(1)} collective-permute-done((f32[4,8,1024]{2,1,0:T(8,128)S(1)}, f32[4,8,1024]{2,1,0:T(8,128)S(1)}, u32[]{:S(2)}, u32[]{:S(2)}) %collective-permute-start.8) | collective-permute-done | bytes 131104 | tf_op jit(solution)/shard_map/ppermute | solution.py:428
  28.9 0.9 %collective-permute-done.9.refs_5_ = f32[4,8,1024]{2,1,0:T(8,128)S(1)} collective-permute-done((f32[4,8,1024]{2,1,0:T(8,128)S(1)}, f32[4,8,1024]{2,1,0:T(8,128)S(1)}, u32[]{:S(2)}, u32[]{:S(2)}) %collective-permute-start.9) | collective-permute-done | bytes 131104 | tf_op jit(solution)/shard_map/ppermute | solution.py:428
  29.8 0.0 collective-permute-done.10.refs_6_
  29.8 0.3 merge_eight.1
  30.0 6.7 %collective-permute-start.11 = (f32[8,1024]{1,0:T(8,128)S(1)}, f32[8,1024]{1,0:T(8,128)S(1)}, u32[]{:S(2)}, u32[]{:S(2)}) collective-permute-start(f32[8,1024]{1,0:T(8,128)S(1)} %get-tuple-element.54), channel_id=1, source_target_pairs={{0,128},{8,136},{16,144},{24,152},{32,160},{40,168},{48,176},{56,1... | collective-permute-start | bytes 98312 | tf_op jit(solution)/shard_map/ppermute | solution.py:428
  36.8 0.6 %collective-permute-start.12 = (f32[8,1024]{1,0:T(8,128)S(1)}, f32[8,1024]{1,0:T(8,128)S(1)}, u32[]{:S(2)}, u32[]{:S(2)}) collective-permute-start(f32[8,1024]{1,0:T(8,128)S(1)} %get-tuple-element.55), channel_id=1, source_target_pairs={{0,192},{8,200},{16,208},{24,216},{32,224},{40,232},{48,240},{56,2... | collective-permute-start | bytes 98312 | tf_op jit(solution)/shard_map/ppermute | solution.py:428
  37.4 1.0 %collective-permute-start.13 = (f32[8,1024]{1,0:T(8,128)S(1)}, f32[8,1024]{1,0:T(8,128)S(1)}, u32[]{:S(2)}, u32[]{:S(2)}) collective-permute-start(f32[8,1024]{1,0:T(8,128)S(1)} %get-tuple-element.56), channel_id=1, source_target_pairs={{0,64},{8,72},{16,80},{24,88},{32,96},{40,104},{48,112},{56,120},{... | collective-permute-start | bytes 98312 | tf_op jit(solution)/shard_map/ppermute | solution.py:428
  38.4 0.3 collective-permute-done.11.refs_0_
  38.7 4.2 %collective-permute-done.12.refs_1_ = f32[8,1024]{1,0:T(8,128)S(1)} collective-permute-done((f32[8,1024]{1,0:T(8,128)S(1)}, f32[8,1024]{1,0:T(8,128)S(1)}, u32[]{:S(2)}, u32[]{:S(2)}) %collective-permute-start.12) | collective-permute-done | bytes 32800 | tf_op jit(solution)/shard_map/ppermute | solution.py:428
  42.8 0.0 collective-permute-done.13.refs_2_
  42.8 0.7 %merge_four.1 = f32[4,2,1024]{2,1,0:T(2,128)} custom-call(f32[8,1024]{1,0:T(8,128)S(1)} %collective-permute-done.11.refs_0_, f32[8,1024]{1,0:T(8,128)S(1)} %collective-permute-done.12.refs_1_, f32[8,1024]{1,0:T(8,128)S(1)} %collective-permute-done.13.refs_2_, f32[8,1024]{1,0:T(8,128)S(1)} %get-tuple-element.57.refs_3_, f32[8,1024]{1,0:T(8,128)S(1)} %get-tuple-element.58.refs_4_), custom_call_target="tpu_custom_call" | custom-call | tf_op jit(solution)/shard_map/merge_four/pallas_call | solution.py:416
Async XLA Ops:
  1.2 8.5 %collective-permute-start.2 = (f32[64,1024]{1,0:T(8,128)S(1)}, f32[64,1024]{1,0:T(8,128)S(1)}, u32[]{:S(2)}, u32[]{:S(2)}) collective-permute-start(f32[64,1024]{1,0:T(8,128)S(1)} %get-tuple-element.38), channel_id=1, source_target_pairs={{0,1},{1,0},{2,3},{3,2},{4,5},{5,4},{6,7},{7,6},{8,16},{9,17},{10,... | collective-permute-start | bytes 786440 | tf_op jit(solution)/shard_map/ppermute | solution.py:443
  1.3 9.2 %collective-permute-start.3 = (f32[64,1024]{1,0:T(8,128)S(1)}, f32[64,1024]{1,0:T(8,128)S(1)}, u32[]{:S(2)}, u32[]{:S(2)}) collective-permute-start(f32[64,1024]{1,0:T(8,128)S(1)} %get-tuple-element.39), channel_id=1, source_target_pairs={{0,8},{8,0},{16,24},{24,16},{32,40},{40,32},{48,56},{56,48},{64,72... | collective-permute-start | bytes 786440 | tf_op jit(solution)/shard_map/ppermute | solution.py:428
  4.4 4.1 %collective-permute-start = (f32[4,1024]{1,0:T(4,128)S(1)}, f32[4,1024]{1,0:T(4,128)S(1)}, u32[]{:S(2)}, u32[]{:S(2)}) collective-permute-start(f32[4,1024]{1,0:T(4,128)S(1)} %get-tuple-element.35), channel_id=1, source_target_pairs={{0,1},{1,0},{2,3},{3,2},{4,5},{5,4},{6,7},{7,6},{8,9},{9,8},{10,11... | collective-permute-start | bytes 49160 | tf_op jit(solution)/shard_map/ppermute | solution.py:428
  4.4 4.1 %collective-permute-start.1 = (f32[4,1024]{1,0:T(4,128)S(1)}, f32[4,1024]{1,0:T(4,128)S(1)}, u32[]{:S(2)}, u32[]{:S(2)}) collective-permute-start(f32[4,1024]{1,0:T(4,128)S(1)} %get-tuple-element.36), channel_id=1, source_target_pairs={{0,8},{1,2},{2,1},{3,4},{4,3},{5,6},{6,5},{7,15},{8,0},{9,10},{10,... | collective-permute-start | bytes 49160 | tf_op jit(solution)/shard_map/ppermute | solution.py:443
  11.4 9.8 %collective-permute-start.4 = (f32[4,8,1024]{2,1,0:T(8,128)S(1)}, f32[4,8,1024]{2,1,0:T(8,128)S(1)}, u32[]{:S(2)}, u32[]{:S(2)}) collective-permute-start(f32[4,8,1024]{2,1,0:T(8,128)S(1)} %get-tuple-element.45), channel_id=1, source_target_pairs={{0,8},{8,0},{16,24},{24,16},{32,40},{40,32},{48,56},{56,48},{64,72... | collective-permute-start | bytes 393224 | tf_op jit(solution)/shard_map/ppermute | solution.py:428
  13.3 9.5 %collective-permute-start.5 = (f32[4,8,1024]{2,1,0:T(8,128)S(1)}, f32[4,8,1024]{2,1,0:T(8,128)S(1)}, u32[]{:S(2)}, u32[]{:S(2)}) collective-permute-start(f32[4,8,1024]{2,1,0:T(8,128)S(1)} %get-tuple-element.46), channel_id=1, source_target_pairs={{0,56},{8,48},{16,40},{24,32},{32,24},{40,16},{48,8},{56,0},{64,12... | collective-permute-start | bytes 393224 | tf_op jit(solution)/shard_map/ppermute | solution.py:428
  17.0 8.3 %collective-permute-start.6 = (f32[4,8,1024]{2,1,0:T(8,128)S(1)}, f32[4,8,1024]{2,1,0:T(8,128)S(1)}, u32[]{:S(2)}, u32[]{:S(2)}) collective-permute-start(f32[4,8,1024]{2,1,0:T(8,128)S(1)} %get-tuple-element.47), channel_id=1, source_target_pairs={{0,24},{8,16},{16,8},{24,0},{32,56},{40,48},{48,40},{56,32},{64,88... | collective-permute-start | bytes 393224 | tf_op jit(solution)/shard_map/ppermute | solution.py:428
  17.8 7.4 %collective-permute-start.7 = (f32[4,8,1024]{2,1,0:T(8,128)S(1)}, f32[4,8,1024]{2,1,0:T(8,128)S(1)}, u32[]{:S(2)}, u32[]{:S(2)}) collective-permute-start(f32[4,8,1024]{2,1,0:T(8,128)S(1)} %get-tuple-element.48), channel_id=1, source_target_pairs={{0,40},{8,32},{16,56},{24,48},{32,8},{40,0},{48,24},{56,16},{64,10... | collective-permute-start | bytes 393224 | tf_op jit(solution)/shard_map/ppermute | solution.py:428
  18.3 10.6 %collective-permute-start.8 = (f32[4,8,1024]{2,1,0:T(8,128)S(1)}, f32[4,8,1024]{2,1,0:T(8,128)S(1)}, u32[]{:S(2)}, u32[]{:S(2)}) collective-permute-start(f32[4,8,1024]{2,1,0:T(8,128)S(1)} %get-tuple-element.49), channel_id=1, source_target_pairs={{0,16},{8,24},{16,0},{24,8},{32,48},{40,56},{48,32},{56,40},{64,80... | collective-permute-start | bytes 393224 | tf_op jit(solution)/shard_map/ppermute | solution.py:428
  21.2 8.5 %collective-permute-start.9 = (f32[4,8,1024]{2,1,0:T(8,128)S(1)}, f32[4,8,1024]{2,1,0:T(8,128)S(1)}, u32[]{:S(2)}, u32[]{:S(2)}) collective-permute-start(f32[4,8,1024]{2,1,0:T(8,128)S(1)} %get-tuple-element.50), channel_id=1, source_target_pairs={{0,48},{8,56},{16,32},{24,40},{32,16},{40,24},{48,0},{56,8},{64,11... | collective-permute-start | bytes 393224 | tf_op jit(solution)/shard_map/ppermute | solution.py:428
  22.7 7.0 %collective-permute-start.10 = (f32[4,8,1024]{2,1,0:T(8,128)S(1)}, f32[4,8,1024]{2,1,0:T(8,128)S(1)}, u32[]{:S(2)}, u32[]{:S(2)}) collective-permute-start(f32[4,8,1024]{2,1,0:T(8,128)S(1)} %get-tuple-element.51), channel_id=1, source_target_pairs={{0,32},{8,40},{16,48},{24,56},{32,0},{40,8},{48,16},{56,24},{64,96... | collective-permute-start | bytes 393224 | tf_op jit(solution)/shard_map/ppermute | solution.py:428
  30.0 8.6 %collective-permute-start.11 = (f32[8,1024]{1,0:T(8,128)S(1)}, f32[8,1024]{1,0:T(8,128)S(1)}, u32[]{:S(2)}, u32[]{:S(2)}) collective-permute-start(f32[8,1024]{1,0:T(8,128)S(1)} %get-tuple-element.54), channel_id=1, source_target_pairs={{0,128},{8,136},{16,144},{24,152},{32,160},{40,168},{48,176},{56,1... | collective-permute-start | bytes 98312 | tf_op jit(solution)/shard_map/ppermute | solution.py:428
  36.8 6.0 %collective-permute-start.12 = (f32[8,1024]{1,0:T(8,128)S(1)}, f32[8,1024]{1,0:T(8,128)S(1)}, u32[]{:S(2)}, u32[]{:S(2)}) collective-permute-start(f32[8,1024]{1,0:T(8,128)S(1)} %get-tuple-element.55), channel_id=1, source_target_pairs={{0,192},{8,200},{16,208},{24,216},{32,224},{40,232},{48,240},{56,2... | collective-permute-start | bytes 98312 | tf_op jit(solution)/shard_map/ppermute | solution.py:428
  37.4 5.4 %collective-permute-start.13 = (f32[8,1024]{1,0:T(8,128)S(1)}, f32[8,1024]{1,0:T(8,128)S(1)}, u32[]{:S(2)}, u32[]{:S(2)}) collective-permute-start(f32[8,1024]{1,0:T(8,128)S(1)} %get-tuple-element.56), channel_id=1, source_target_pairs={{0,64},{8,72},{16,80},{24,88},{32,96},{40,104},{48,112},{56,120},{... | collective-permute-start | bytes 98312 | tf_op jit(solution)/shard_map/ppermute | solution.py:428

commit v5 on v4

--- a/solution.py
+++ b/solution.py
@@ -319,7 +319,7 @@
                 s[4 * half + piece, i, :, cols] = value
         return carry
 
-    lax.fori_loop(0, 2 * chunks, part, 0)
+    lax.fori_loop(0, 2 * chunks, part, 0, unroll=2)
     place = slab & 7
     for j in range(8):
         for i in range(4):

time: 44 us -> 43.9 us (level)
  no operation moved by 1% of the time
where the time goes in v5:
time: 43.9 us; the launch traced here: 43.4 us
  starting transfers between devices  24.3 us (55%)
  waiting for transfers between devices  11.5 us (26%)
  Pallas kernels  7.6 us (17%)
    ppermute x12, starting transfers between devices, swap(): return lax.ppermute(block, axis, [(i, i ^ step) for i in range(count)])  23.5 us
    ppermute x12, waiting for transfers between devices, swap(): return lax.ppermute(block, axis, [(i, i ^ step) for i in range(count)])  11.5 us
    pallas_call x1, Pallas kernels, look(): pl.pallas_call(lambda *refs: look_kernel(spacing, *refs), out_shape=[jax....  3.42 us
    pallas_call x1, Pallas kernels, faces(): pl.pallas_call(faces_kernel, out_shape=[jax.ShapeDtypeStruct((rows, line)...  1.15 us
    pallas_call x1, Pallas kernels, slopes(): pl.pallas_call(slopes_kernel, out_shape=[jax.ShapeDtypeStruct(density.sha...  1.15 us
    pallas_call x1, Pallas kernels, edges(): pl.pallas_call(edges_kernel, out_shape=[jax.ShapeDtypeStruct((4, 8, line)...  0.91 us
  transfers between devices with their start and end apart: 14, of which 6 were waited for; matrix products, arithmetic and copies ran while one was open for 0% of the time, Pallas kernels for 11%

profile of v5, /device:TPU:2, one launch (start us, length us, event | category | flops | bytes accessed | tf_op | source)
XLA Modules:
  0.0 43.4 jit_solution(7303097836384140748)
XLA Ops:
  0.0 1.2 %faces.1 = (f32[64,1024]{1,0:T(8,128)S(1)}, f32[64,1024]{1,0:T(8,128)S(1)}, f32[4,1024]{1,0:T(4,128)S(1)}, f32[4,1024]{1,0:T(4,128)S(1)}, s32[3,8,128]{2,1,0:T(8,128)S(1)}) custom-call(f32[4,64,1024]{2,1,0:T(8,128)} %refs_0_.1, bf16[4,256]{1,0:T(4,128)(2,1)} %t_ref.1), custom_call_target="tpu_custom_call" | custom-call | tf_op jit(solution)/shard_map/faces/pallas_call | solution.py:61
  1.2 0.1 collective-permute-start.2
  1.3 3.1 %collective-permute-start.3 = (f32[64,1024]{1,0:T(8,128)S(1)}, f32[64,1024]{1,0:T(8,128)S(1)}, u32[]{:S(2)}, u32[]{:S(2)}) collective-permute-start(f32[64,1024]{1,0:T(8,128)S(1)} %get-tuple-element.39), channel_id=1, source_target_pairs={{0,8},{8,0},{16,24},{24,16},{32,40},{40,32},{48,56},{56,48},{64,72... | collective-permute-start | bytes 786440 | tf_op jit(solution)/shard_map/ppermute | solution.py:428
  4.4 0.0 collective-permute-start
  4.4 0.6 %collective-permute-start.1 = (f32[4,1024]{1,0:T(4,128)S(1)}, f32[4,1024]{1,0:T(4,128)S(1)}, u32[]{:S(2)}, u32[]{:S(2)}) collective-permute-start(f32[4,1024]{1,0:T(4,128)S(1)} %get-tuple-element.36), channel_id=1, source_target_pairs={{0,8},{1,2},{2,1},{3,4},{4,3},{5,6},{6,5},{7,15},{8,0},{9,10},{10,... | collective-permute-start | bytes 49160 | tf_op jit(solution)/shard_map/ppermute | solution.py:443
  5.1 3.4 %look.1 = (f32[4,80,1024]{2,1,0:T(8,128)S(1)}, f32[4,3,64,1024]{3,2,1,0:T(8,128)S(1)}, f32[64,1024]{1,0:T(8,128)S(1)}, s32[64,1024]{1,0:T(8,128)S(1)}) custom-call(f32[4,64,1024]{2,1,0:T(8,128)} %refs_0_.1, s32[4,64,1024]{2,1,0:T(8,128)} %refs_1_.1, s32[64,1024]{1,0:T(8,128)} %refs_2_.1, s32[3,8,128]{2,1,0:T(8,128)S(1)} %get-tuple-element.32.refs_3_), custom_call_target="tpu_custom_call" | custom-call | flops 13107200 | bytes 3145728 | tf_op jit(solution)/shard_map/look/pallas_call | solution.py:169
  8.5 0.0 collective-permute-done.ya_ref
  8.5 0.0 collective-permute-done.1.yb_ref
  8.5 1.2 %slopes.1 = (f32[4,80,1024]{2,1,0:T(8,128)S(1)}, f32[3,64,1024]{2,1,0:T(8,128)S(1)}, f32[2,64,1024]{2,1,0:T(8,128)S(1)}, f32[2,64,1024]{2,1,0:T(8,128)S(1)}) custom-call(f32[4,80,1024]{2,1,0:T(8,128)S(1)} %get-tuple-element.33.d_in, f32[4,3,64,1024]{3,2,1,0:T(8,128)S(1)} %get-tuple-element.34.w_ref, ...), custom_call_target="tpu_custom_call", output_to_operand_aliasing={{0}: (0, {})} | custom-call | flops 13107200 | bytes 3145728 | tf_op jit(solution)/shard_map/slopes/pallas_call | solution.py:251
  9.7 0.0 collective-permute-done.2.zb_ref
  9.7 0.7 %collective-permute-done.3.za_ref = f32[64,1024]{1,0:T(8,128)S(1)} collective-permute-done((f32[64,1024]{1,0:T(8,128)S(1)}, f32[64,1024]{1,0:T(8,128)S(1)}, u32[]{:S(2)}, u32[]{:S(2)}) %collective-permute-start.3) | collective-permute-done | bytes 262176 | tf_op jit(solution)/shard_map/ppermute | solution.py:428
  10.4 0.9 %edges.1 = (f32[4,8,1024]{2,1,0:T(8,128)S(1)}, f32[4,8,1024]{2,1,0:T(8,128)S(1)}, f32[4,8,1024]{2,1,0:T(8,128)S(1)}, f32[4,8,1024]{2,1,0:T(8,128)S(1)}, f32[4,8,...) custom-call(f32[4,80,1024]{2,1,0:T(8,128)S(1)} %get-tuple-element.37, ...), custom_call_target="tpu_custom_call" | custom-call | flops 10485760 | bytes 1048576 | tf_op jit(solution)/shard_map/edges/pallas_call | solution.py:334
  11.3 1.8 %collective-permute-start.4 = (f32[4,8,1024]{2,1,0:T(8,128)S(1)}, f32[4,8,1024]{2,1,0:T(8,128)S(1)}, u32[]{:S(2)}, u32[]{:S(2)}) collective-permute-start(f32[4,8,1024]{2,1,0:T(8,128)S(1)} %get-tuple-element.45), channel_id=1, source_target_pairs={{0,8},{8,0},{16,24},{24,16},{32,40},{40,32},{48,56},{56,48},{64,72... | collective-permute-start | bytes 393224 | tf_op jit(solution)/shard_map/ppermute | solution.py:428
  13.2 3.7 %collective-permute-start.5 = (f32[4,8,1024]{2,1,0:T(8,128)S(1)}, f32[4,8,1024]{2,1,0:T(8,128)S(1)}, u32[]{:S(2)}, u32[]{:S(2)}) collective-permute-start(f32[4,8,1024]{2,1,0:T(8,128)S(1)} %get-tuple-element.46), channel_id=1, source_target_pairs={{0,56},{8,48},{16,40},{24,32},{32,24},{40,16},{48,8},{56,0},{64,12... | collective-permute-start | bytes 393224 | tf_op jit(solution)/shard_map/ppermute | solution.py:428
  16.9 0.9 %collective-permute-start.6 = (f32[4,8,1024]{2,1,0:T(8,128)S(1)}, f32[4,8,1024]{2,1,0:T(8,128)S(1)}, u32[]{:S(2)}, u32[]{:S(2)}) collective-permute-start(f32[4,8,1024]{2,1,0:T(8,128)S(1)} %get-tuple-element.47), channel_id=1, source_target_pairs={{0,24},{8,16},{16,8},{24,0},{32,56},{40,48},{48,40},{56,32},{64,88... | collective-permute-start | bytes 393224 | tf_op jit(solution)/shard_map/ppermute | solution.py:428
  17.8 0.4 %collective-permute-start.7 = (f32[4,8,1024]{2,1,0:T(8,128)S(1)}, f32[4,8,1024]{2,1,0:T(8,128)S(1)}, u32[]{:S(2)}, u32[]{:S(2)}) collective-permute-start(f32[4,8,1024]{2,1,0:T(8,128)S(1)} %get-tuple-element.48), channel_id=1, source_target_pairs={{0,40},{8,32},{16,56},{24,48},{32,8},{40,0},{48,24},{56,16},{64,10... | collective-permute-start | bytes 393224 | tf_op jit(solution)/shard_map/ppermute | solution.py:428
  18.2 2.9 %collective-permute-start.8 = (f32[4,8,1024]{2,1,0:T(8,128)S(1)}, f32[4,8,1024]{2,1,0:T(8,128)S(1)}, u32[]{:S(2)}, u32[]{:S(2)}) collective-permute-start(f32[4,8,1024]{2,1,0:T(8,128)S(1)} %get-tuple-element.49), channel_id=1, source_target_pairs={{0,16},{8,24},{16,0},{24,8},{32,48},{40,56},{48,32},{56,40},{64,80... | collective-permute-start | bytes 393224 | tf_op jit(solution)/shard_map/ppermute | solution.py:428
  21.1 0.0 collective-permute-done.4.refs_0_
  21.1 1.5 %collective-permute-start.9 = (f32[4,8,1024]{2,1,0:T(8,128)S(1)}, f32[4,8,1024]{2,1,0:T(8,128)S(1)}, u32[]{:S(2)}, u32[]{:S(2)}) collective-permute-start(f32[4,8,1024]{2,1,0:T(8,128)S(1)} %get-tuple-element.50), channel_id=1, source_target_pairs={{0,48},{8,56},{16,32},{24,40},{32,16},{40,24},{48,0},{56,8},{64,11... | collective-permute-start | bytes 393224 | tf_op jit(solution)/shard_map/ppermute | solution.py:428
  22.6 0.0 collective-permute-done.5.refs_1_
  22.6 0.8 %collective-permute-start.10 = (f32[4,8,1024]{2,1,0:T(8,128)S(1)}, f32[4,8,1024]{2,1,0:T(8,128)S(1)}, u32[]{:S(2)}, u32[]{:S(2)}) collective-permute-start(f32[4,8,1024]{2,1,0:T(8,128)S(1)} %get-tuple-element.51), channel_id=1, source_target_pairs={{0,32},{8,40},{16,48},{24,56},{32,0},{40,8},{48,16},{56,24},{64,96... | collective-permute-start | bytes 393224 | tf_op jit(solution)/shard_map/ppermute | solution.py:428
  23.4 1.8 %collective-permute-done.6.refs_2_ = f32[4,8,1024]{2,1,0:T(8,128)S(1)} collective-permute-done((f32[4,8,1024]{2,1,0:T(8,128)S(1)}, f32[4,8,1024]{2,1,0:T(8,128)S(1)}, u32[]{:S(2)}, u32[]{:S(2)}) %collective-permute-start.6) | collective-permute-done | bytes 131104 | tf_op jit(solution)/shard_map/ppermute | solution.py:428
  25.2 0.0 collective-permute-done.7.refs_3_
  25.2 3.6 %collective-permute-done.8.refs_4_ = f32[4,8,1024]{2,1,0:T(8,128)S(1)} collective-permute-done((f32[4,8,1024]{2,1,0:T(8,128)S(1)}, f32[4,8,1024]{2,1,0:T(8,128)S(1)}, u32[]{:S(2)}, u32[]{:S(2)}) %collective-permute-start.8) | collective-permute-done | bytes 131104 | tf_op jit(solution)/shard_map/ppermute | solution.py:428
  28.8 0.9 %collective-permute-done.9.refs_5_ = f32[4,8,1024]{2,1,0:T(8,128)S(1)} collective-permute-done((f32[4,8,1024]{2,1,0:T(8,128)S(1)}, f32[4,8,1024]{2,1,0:T(8,128)S(1)}, u32[]{:S(2)}, u32[]{:S(2)}) %collective-permute-start.9) | collective-permute-done | bytes 131104 | tf_op jit(solution)/shard_map/ppermute | solution.py:428
  29.7 0.0 collective-permute-done.10.refs_6_
  29.7 0.3 merge_eight.1
  30.0 6.7 %collective-permute-start.11 = (f32[8,1024]{1,0:T(8,128)S(1)}, f32[8,1024]{1,0:T(8,128)S(1)}, u32[]{:S(2)}, u32[]{:S(2)}) collective-permute-start(f32[8,1024]{1,0:T(8,128)S(1)} %get-tuple-element.54), channel_id=1, source_target_pairs={{0,128},{8,136},{16,144},{24,152},{32,160},{40,168},{48,176},{56,1... | collective-permute-start | bytes 98312 | tf_op jit(solution)/shard_map/ppermute | solution.py:428
  36.7 0.6 %collective-permute-start.12 = (f32[8,1024]{1,0:T(8,128)S(1)}, f32[8,1024]{1,0:T(8,128)S(1)}, u32[]{:S(2)}, u32[]{:S(2)}) collective-permute-start(f32[8,1024]{1,0:T(8,128)S(1)} %get-tuple-element.55), channel_id=1, source_target_pairs={{0,192},{8,200},{16,208},{24,216},{32,224},{40,232},{48,240},{56,2... | collective-permute-start | bytes 98312 | tf_op jit(solution)/shard_map/ppermute | solution.py:428
  37.3 1.0 %collective-permute-start.13 = (f32[8,1024]{1,0:T(8,128)S(1)}, f32[8,1024]{1,0:T(8,128)S(1)}, u32[]{:S(2)}, u32[]{:S(2)}) collective-permute-start(f32[8,1024]{1,0:T(8,128)S(1)} %get-tuple-element.56), channel_id=1, source_target_pairs={{0,64},{8,72},{16,80},{24,88},{32,96},{40,104},{48,112},{56,120},{... | collective-permute-start | bytes 98312 | tf_op jit(solution)/shard_map/ppermute | solution.py:428
  38.3 0.3 collective-permute-done.11.refs_0_
  38.6 4.2 %collective-permute-done.12.refs_1_ = f32[8,1024]{1,0:T(8,128)S(1)} collective-permute-done((f32[8,1024]{1,0:T(8,128)S(1)}, f32[8,1024]{1,0:T(8,128)S(1)}, u32[]{:S(2)}, u32[]{:S(2)}) %collective-permute-start.12) | collective-permute-done | bytes 32800 | tf_op jit(solution)/shard_map/ppermute | solution.py:428
  42.7 0.0 collective-permute-done.13.refs_2_
  42.8 0.7 %merge_four.1 = f32[4,2,1024]{2,1,0:T(2,128)} custom-call(f32[8,1024]{1,0:T(8,128)S(1)} %collective-permute-done.11.refs_0_, f32[8,1024]{1,0:T(8,128)S(1)} %collective-permute-done.12.refs_1_, f32[8,1024]{1,0:T(8,128)S(1)} %collective-permute-done.13.refs_2_, f32[8,1024]{1,0:T(8,128)S(1)} %get-tuple-element.57.refs_3_, f32[8,1024]{1,0:T(8,128)S(1)} %get-tuple-element.58.refs_4_), custom_call_target="tpu_custom_call" | custom-call | tf_op jit(solution)/shard_map/merge_four/pallas_call | solution.py:416
Async XLA Ops:
  1.2 8.5 %collective-permute-start.2 = (f32[64,1024]{1,0:T(8,128)S(1)}, f32[64,1024]{1,0:T(8,128)S(1)}, u32[]{:S(2)}, u32[]{:S(2)}) collective-permute-start(f32[64,1024]{1,0:T(8,128)S(1)} %get-tuple-element.38), channel_id=1, source_target_pairs={{0,1},{1,0},{2,3},{3,2},{4,5},{5,4},{6,7},{7,6},{8,16},{9,17},{10,... | collective-permute-start | bytes 786440 | tf_op jit(solution)/shard_map/ppermute | solution.py:443
  1.3 9.2 %collective-permute-start.3 = (f32[64,1024]{1,0:T(8,128)S(1)}, f32[64,1024]{1,0:T(8,128)S(1)}, u32[]{:S(2)}, u32[]{:S(2)}) collective-permute-start(f32[64,1024]{1,0:T(8,128)S(1)} %get-tuple-element.39), channel_id=1, source_target_pairs={{0,8},{8,0},{16,24},{24,16},{32,40},{40,32},{48,56},{56,48},{64,72... | collective-permute-start | bytes 786440 | tf_op jit(solution)/shard_map/ppermute | solution.py:428
  4.4 4.1 %collective-permute-start = (f32[4,1024]{1,0:T(4,128)S(1)}, f32[4,1024]{1,0:T(4,128)S(1)}, u32[]{:S(2)}, u32[]{:S(2)}) collective-permute-start(f32[4,1024]{1,0:T(4,128)S(1)} %get-tuple-element.35), channel_id=1, source_target_pairs={{0,1},{1,0},{2,3},{3,2},{4,5},{5,4},{6,7},{7,6},{8,9},{9,8},{10,11... | collective-permute-start | bytes 49160 | tf_op jit(solution)/shard_map/ppermute | solution.py:428
  4.4 4.1 %collective-permute-start.1 = (f32[4,1024]{1,0:T(4,128)S(1)}, f32[4,1024]{1,0:T(4,128)S(1)}, u32[]{:S(2)}, u32[]{:S(2)}) collective-permute-start(f32[4,1024]{1,0:T(4,128)S(1)} %get-tuple-element.36), channel_id=1, source_target_pairs={{0,8},{1,2},{2,1},{3,4},{4,3},{5,6},{6,5},{7,15},{8,0},{9,10},{10,... | collective-permute-start | bytes 49160 | tf_op jit(solution)/shard_map/ppermute | solution.py:443
  11.3 9.8 %collective-permute-start.4 = (f32[4,8,1024]{2,1,0:T(8,128)S(1)}, f32[4,8,1024]{2,1,0:T(8,128)S(1)}, u32[]{:S(2)}, u32[]{:S(2)}) collective-permute-start(f32[4,8,1024]{2,1,0:T(8,128)S(1)} %get-tuple-element.45), channel_id=1, source_target_pairs={{0,8},{8,0},{16,24},{24,16},{32,40},{40,32},{48,56},{56,48},{64,72... | collective-permute-start | bytes 393224 | tf_op jit(solution)/shard_map/ppermute | solution.py:428
  13.2 9.5 %collective-permute-start.5 = (f32[4,8,1024]{2,1,0:T(8,128)S(1)}, f32[4,8,1024]{2,1,0:T(8,128)S(1)}, u32[]{:S(2)}, u32[]{:S(2)}) collective-permute-start(f32[4,8,1024]{2,1,0:T(8,128)S(1)} %get-tuple-element.46), channel_id=1, source_target_pairs={{0,56},{8,48},{16,40},{24,32},{32,24},{40,16},{48,8},{56,0},{64,12... | collective-permute-start | bytes 393224 | tf_op jit(solution)/shard_map/ppermute | solution.py:428
  16.9 8.3 %collective-permute-start.6 = (f32[4,8,1024]{2,1,0:T(8,128)S(1)}, f32[4,8,1024]{2,1,0:T(8,128)S(1)}, u32[]{:S(2)}, u32[]{:S(2)}) collective-permute-start(f32[4,8,1024]{2,1,0:T(8,128)S(1)} %get-tuple-element.47), channel_id=1, source_target_pairs={{0,24},{8,16},{16,8},{24,0},{32,56},{40,48},{48,40},{56,32},{64,88... | collective-permute-start | bytes 393224 | tf_op jit(solution)/shard_map/ppermute | solution.py:428
  17.8 7.4 %collective-permute-start.7 = (f32[4,8,1024]{2,1,0:T(8,128)S(1)}, f32[4,8,1024]{2,1,0:T(8,128)S(1)}, u32[]{:S(2)}, u32[]{:S(2)}) collective-permute-start(f32[4,8,1024]{2,1,0:T(8,128)S(1)} %get-tuple-element.48), channel_id=1, source_target_pairs={{0,40},{8,32},{16,56},{24,48},{32,8},{40,0},{48,24},{56,16},{64,10... | collective-permute-start | bytes 393224 | tf_op jit(solution)/shard_map/ppermute | solution.py:428
  18.2 10.6 %collective-permute-start.8 = (f32[4,8,1024]{2,1,0:T(8,128)S(1)}, f32[4,8,1024]{2,1,0:T(8,128)S(1)}, u32[]{:S(2)}, u32[]{:S(2)}) collective-permute-start(f32[4,8,1024]{2,1,0:T(8,128)S(1)} %get-tuple-element.49), channel_id=1, source_target_pairs={{0,16},{8,24},{16,0},{24,8},{32,48},{40,56},{48,32},{56,40},{64,80... | collective-permute-start | bytes 393224 | tf_op jit(solution)/shard_map/ppermute | solution.py:428
  21.1 8.5 %collective-permute-start.9 = (f32[4,8,1024]{2,1,0:T(8,128)S(1)}, f32[4,8,1024]{2,1,0:T(8,128)S(1)}, u32[]{:S(2)}, u32[]{:S(2)}) collective-permute-start(f32[4,8,1024]{2,1,0:T(8,128)S(1)} %get-tuple-element.50), channel_id=1, source_target_pairs={{0,48},{8,56},{16,32},{24,40},{32,16},{40,24},{48,0},{56,8},{64,11... | collective-permute-start | bytes 393224 | tf_op jit(solution)/shard_map/ppermute | solution.py:428
  22.6 7.0 %collective-permute-start.10 = (f32[4,8,1024]{2,1,0:T(8,128)S(1)}, f32[4,8,1024]{2,1,0:T(8,128)S(1)}, u32[]{:S(2)}, u32[]{:S(2)}) collective-permute-start(f32[4,8,1024]{2,1,0:T(8,128)S(1)} %get-tuple-element.51), channel_id=1, source_target_pairs={{0,32},{8,40},{16,48},{24,56},{32,0},{40,8},{48,16},{56,24},{64,96... | collective-permute-start | bytes 393224 | tf_op jit(solution)/shard_map/ppermute | solution.py:428
  30.0 8.6 %collective-permute-start.11 = (f32[8,1024]{1,0:T(8,128)S(1)}, f32[8,1024]{1,0:T(8,128)S(1)}, u32[]{:S(2)}, u32[]{:S(2)}) collective-permute-start(f32[8,1024]{1,0:T(8,128)S(1)} %get-tuple-element.54), channel_id=1, source_target_pairs={{0,128},{8,136},{16,144},{24,152},{32,160},{40,168},{48,176},{56,1... | collective-permute-start | bytes 98312 | tf_op jit(solution)/shard_map/ppermute | solution.py:428
  36.7 6.0 %collective-permute-start.12 = (f32[8,1024]{1,0:T(8,128)S(1)}, f32[8,1024]{1,0:T(8,128)S(1)}, u32[]{:S(2)}, u32[]{:S(2)}) collective-permute-start(f32[8,1024]{1,0:T(8,128)S(1)} %get-tuple-element.55), channel_id=1, source_target_pairs={{0,192},{8,200},{16,208},{24,216},{32,224},{40,232},{48,240},{56,2... | collective-permute-start | bytes 98312 | tf_op jit(solution)/shard_map/ppermute | solution.py:428
  37.3 5.4 %collective-permute-start.13 = (f32[8,1024]{1,0:T(8,128)S(1)}, f32[8,1024]{1,0:T(8,128)S(1)}, u32[]{:S(2)}, u32[]{:S(2)}) collective-permute-start(f32[8,1024]{1,0:T(8,128)S(1)} %get-tuple-element.56), channel_id=1, source_target_pairs={{0,64},{8,72},{16,80},{24,88},{32,96},{40,104},{48,112},{56,120},{... | collective-permute-start | bytes 98312 | tf_op jit(solution)/shard_map/ppermute | solution.py:428
